TPU v7x, 32 devices: a whole 2x2x4 slice. The times are simulated.
32 devices in a mesh: ctx: 8 (over y, x, core), fsdp: 4 (over z).
Axes of the slice: x: 2, y: 2, z: 4, core: 2. Of those that a mesh axis runs over, the one named last changes fastest.
Arguments:
- tokens: bfloat16 [4096, 960], P(('ctx', 'fsdp')), may hold values from -6 to 6
- pair_order: int32 [32], replicated, may hold values from 0 to 31, each once
- gain_attn: bfloat16 [960], P('fsdp'), may hold values from 0.5 to 1.5
- gain_mlp: bfloat16 [960], P('fsdp'), may hold values from 0.5 to 1.5
- w_query: bfloat16 [960, 960], P('fsdp'), may hold values from -0.3125 to 0.3125
- w_key: bfloat16 [960, 320], P('fsdp'), may hold values from -0.3125 to 0.3125
- w_value: bfloat16 [960, 320], P('fsdp'), may hold values from -0.1875 to 0.1875
- w_out: bfloat16 [960, 960], P('fsdp'), may hold values from -0.75 to 0.75
- w_gate: bfloat16 [960, 2560], P('fsdp'), may hold values from -0.1875 to 0.1875
- w_up: bfloat16 [960, 2560], P('fsdp'), may hold values from -0.1875 to 0.1875
- w_down: bfloat16 [2560, 960], P('fsdp'), may hold values from -0.125 to 0.125
- cotangent: bfloat16 [4096, 960], P(('ctx', 'fsdp')), may hold values from -6 to 6
Outputs:
- layer_out: bfloat16 [4096, 960], P(('ctx', 'fsdp'))
- grad_tokens: float32 [4096, 960], P(('ctx', 'fsdp'))
- grad_gain_attn: float32 [960], P('fsdp')
- grad_gain_mlp: float32 [960], P('fsdp')
- grad_w_query: float32 [960, 960], P('fsdp')
- grad_w_key: float32 [960, 320], P('fsdp')
- grad_w_value: float32 [960, 320], P('fsdp')
- grad_w_out: float32 [960, 960], P('fsdp')
- grad_w_gate: float32 [960, 2560], P('fsdp')
- grad_w_up: float32 [960, 2560], P('fsdp')
- grad_w_down: float32 [2560, 960], P('fsdp')
Inputs may be any that keep to these rules, and one draw needn't show every extreme that they name: Slot d holds sequence blocks pair_order[d] and 63 - pair_order[d]; each value appears once.
All inputs are finite; a program needn't handle non-finite values.
Results may differ from a plain program's by a relative error of at most 0.025.
Values may be sent and summed in bfloat16 or wider, within the bound.
No kernel may reach another device: no remote copies, remote signals or barrier semaphores. Data moves between devices by JAX's collectives and lax.ppermute only.
A program may use at most 256 MiB of HBM per device.

v0:
```python
import math

import jax
import jax.numpy as jnp
from jax import lax
from jax.sharding import PartitionSpec as P

HEADS = 15
KV_HEADS = 5
HEAD = 64


epsilon = 1e-05
base_theta = 100000.0
far_below = -1e30


def positions(pair_order, local_rows):
    devices = pair_order.shape[0]
    half_rows = local_rows // 2
    first_block = pair_order * half_rows
    second_block = (2 * devices - 1 - pair_order) * half_rows
    offsets = jnp.arange(half_rows, dtype=jnp.int32)
    placed = jnp.concatenate(
        [first_block[:, None] + offsets[None, :], second_block[:, None] + offsets[None, :]], axis=1
    )
    return placed.reshape(-1)


def rotate(matrix, places, heads, sign):
    width = matrix.shape[1] // heads
    half_width = width // 2
    freqs = base_theta ** (-2.0 * jnp.arange(half_width, dtype=jnp.float32) / width)
    angles = places.astype(jnp.float32)[:, None] * freqs[None, :]
    cosine = jnp.cos(angles)[:, None, :]
    sine = sign * jnp.sin(angles)[:, None, :]
    split = matrix.reshape(matrix.shape[0], heads, width)
    front = split[..., :half_width]
    back = split[..., half_width:]
    turned = jnp.concatenate([front * cosine - back * sine, back * cosine + front * sine], axis=2)
    return turned.reshape(matrix.shape)


def to_groups(matrix, local_rows):
    group = HEADS // KV_HEADS
    shaped = matrix.reshape(local_rows, KV_HEADS, group, HEAD)
    return shaped.transpose(1, 2, 0, 3).reshape(KV_HEADS, group * local_rows, HEAD)


def from_groups(stacked, local_rows):
    group = HEADS // KV_HEADS
    shaped = stacked.reshape(KV_HEADS, group, local_rows, HEAD)
    return shaped.transpose(2, 0, 1, 3).reshape(local_rows, HEADS * HEAD)


def body(
    tokens,
    pair_order,
    gain_attn,
    gain_mlp,
    w_query,
    w_key,
    w_value,
    w_out,
    w_gate,
    w_up,
    w_down,
    cotangent,
):
    local_rows = tokens.shape[0]
    devices = lax.axis_size(("ctx", "fsdp"))
    my_index = lax.axis_index(("ctx", "fsdp"))
    group = HEADS // KV_HEADS
    kv_width = KV_HEADS * HEAD
    total_rows = local_rows * devices
    key_block = total_rows // 16
    scale = HEAD ** (-0.5)
    key_places = positions(pair_order, local_rows)
    own_places = lax.dynamic_slice_in_dim(key_places, my_index * local_rows, local_rows)
    query_places = jnp.tile(own_places, group)
    gathered_w = (
        lax.all_gather(gain_attn, "fsdp", axis=0, tiled=True),
        lax.all_gather(gain_mlp, "fsdp", axis=0, tiled=True),
        lax.all_gather(w_query, "fsdp", axis=0, tiled=True),
        lax.all_gather(w_key, "fsdp", axis=0, tiled=True),
        lax.all_gather(w_value, "fsdp", axis=0, tiled=True),
        lax.all_gather(w_out, "fsdp", axis=0, tiled=True),
        lax.all_gather(w_gate, "fsdp", axis=0, tiled=True),
        lax.all_gather(w_up, "fsdp", axis=0, tiled=True),
        lax.all_gather(w_down, "fsdp", axis=0, tiled=True),
    )
    (
        gain_one,
        gain_two,
        whole_query,
        whole_key,
        whole_value,
        whole_out,
        whole_gate,
        whole_up,
        whole_down,
    ) = gathered_w
    inputs = tokens.astype(jnp.float32)
    inverse_one = lax.rsqrt(jnp.mean(inputs * inputs, axis=1, keepdims=True) + epsilon)
    normal_one = inputs * inverse_one
    hidden_one = (normal_one * gain_one.astype(jnp.float32)[None, :]).astype(jnp.bfloat16)
    query = rotate(
        jnp.dot(hidden_one, whole_query, preferred_element_type=jnp.float32), own_places, HEADS, 1.0
    ).astype(jnp.bfloat16)
    key = rotate(
        jnp.dot(hidden_one, whole_key, preferred_element_type=jnp.float32),
        own_places,
        KV_HEADS,
        1.0,
    ).astype(jnp.bfloat16)
    value = jnp.dot(hidden_one, whole_value, preferred_element_type=jnp.float32).astype(
        jnp.bfloat16
    )
    packed = jnp.concatenate([key, value], axis=1)
    grouped = to_groups(query, local_rows)
    start_state = (
        jnp.zeros((KV_HEADS, group * local_rows, HEAD), jnp.float32),
        jnp.full((KV_HEADS, group * local_rows), far_below, jnp.float32),
        jnp.zeros((KV_HEADS, group * local_rows), jnp.float32),
    )
    gathered_kv = lax.all_gather(packed, ("ctx", "fsdp"), axis=0, tiled=True)
    state = start_state
    count = gathered_kv.shape[0]
    size = math.gcd(count, key_block)
    blocks_kv = gathered_kv.reshape(count // size, size, 2 * kv_width)
    blocks_at = key_places.reshape(count // size, size)

    def forward_one_block(carried, inputs_block):
        accum, running, mass = carried
        block_kv, block_at = inputs_block
        keys = block_kv[:, :kv_width].reshape(size, KV_HEADS, HEAD)
        values = block_kv[:, kv_width:].reshape(size, KV_HEADS, HEAD)
        allowed = (query_places[:, None] >= block_at[None, :])[None]
        scores = (
            jnp.einsum("hqd,khd->hqk", grouped, keys, preferred_element_type=jnp.float32) * scale
        )
        scores = jnp.where(allowed, scores, far_below)
        highest = jnp.maximum(running, jnp.max(scores, axis=2))
        weights = jnp.where(allowed, jnp.exp(scores - highest[:, :, None]), 0.0)
        fade = jnp.exp(running - highest)
        mass = mass * fade + jnp.sum(weights, axis=2)
        accum = accum * fade[:, :, None] + jnp.einsum(
            "hqk,khd->hqd", weights.astype(jnp.bfloat16), values, preferred_element_type=jnp.float32
        )
        return ((accum, highest, mass), None)

    state, unused = lax.scan(forward_one_block, state, (blocks_kv, blocks_at))
    accum, running, mass = state
    log_mass = running + jnp.log(mass)
    attended = from_groups(accum / mass[:, :, None], local_rows)
    attended_low = attended.astype(jnp.bfloat16)
    resid = inputs + jnp.dot(attended_low, whole_out, preferred_element_type=jnp.float32)
    inverse_two = lax.rsqrt(jnp.mean(resid * resid, axis=1, keepdims=True) + epsilon)
    normal_two = resid * inverse_two
    hidden_two = (normal_two * gain_two.astype(jnp.float32)[None, :]).astype(jnp.bfloat16)
    gate = jnp.dot(hidden_two, whole_gate, preferred_element_type=jnp.float32)
    up_part = jnp.dot(hidden_two, whole_up, preferred_element_type=jnp.float32)
    sigmoid_gate = jax.nn.sigmoid(gate)
    activated = gate * sigmoid_gate
    product = (activated * up_part).astype(jnp.bfloat16)
    layer_out = (resid + jnp.dot(product, whole_down, preferred_element_type=jnp.float32)).astype(
        jnp.bfloat16
    )
    grad_down = jnp.einsum("tf,td->fd", product, cotangent, preferred_element_type=jnp.float32)
    grad_product = jnp.einsum(
        "td,fd->tf", cotangent, whole_down, preferred_element_type=jnp.float32
    )
    grad_gate = (
        grad_product * up_part * sigmoid_gate * (1.0 + gate * (1.0 - sigmoid_gate))
    ).astype(jnp.bfloat16)
    grad_up = (grad_product * activated).astype(jnp.bfloat16)
    grad_gate_w = jnp.einsum("td,tf->df", hidden_two, grad_gate, preferred_element_type=jnp.float32)
    grad_up_w = jnp.einsum("td,tf->df", hidden_two, grad_up, preferred_element_type=jnp.float32)
    grad_hidden_two = jnp.einsum(
        "tf,df->td", grad_gate, whole_gate, preferred_element_type=jnp.float32
    ) + jnp.einsum("tf,df->td", grad_up, whole_up, preferred_element_type=jnp.float32)
    grad_gain_two = jnp.sum(grad_hidden_two * normal_two, axis=0)
    grad_normal_two = grad_hidden_two * gain_two.astype(jnp.float32)[None, :]
    grad_resid = inverse_two * (
        grad_normal_two - normal_two * jnp.mean(grad_normal_two * normal_two, axis=1, keepdims=True)
    ) + cotangent.astype(jnp.float32)
    grad_branch = grad_resid.astype(jnp.bfloat16)
    grad_out_w = jnp.einsum(
        "tq,td->qd", attended_low, grad_branch, preferred_element_type=jnp.float32
    )
    grad_attended = jnp.einsum(
        "td,qd->tq", grad_branch, whole_out, preferred_element_type=jnp.float32
    ).astype(jnp.bfloat16)
    row_delta = jnp.sum(
        (grad_attended.astype(jnp.float32) * attended).reshape(local_rows, KV_HEADS, group, HEAD),
        axis=3,
    )
    delta = row_delta.transpose(1, 2, 0).reshape(KV_HEADS, group * local_rows)
    grad_grouped = to_groups(grad_attended, local_rows)
    grad_query_acc = jnp.zeros((KV_HEADS, group * local_rows, HEAD), jnp.float32)
    count = gathered_kv.shape[0]
    backward_size = math.gcd(count, key_block)
    blocks_kv = gathered_kv.reshape(count // backward_size, backward_size, 2 * kv_width)
    blocks_at = key_places.reshape(count // backward_size, backward_size)

    def backward_one_block(carried, inputs_block):
        block_kv, block_at = inputs_block
        keys = block_kv[:, :kv_width].reshape(backward_size, KV_HEADS, HEAD)
        values = block_kv[:, kv_width:].reshape(backward_size, KV_HEADS, HEAD)
        allowed = (query_places[:, None] >= block_at[None, :])[None]
        scores = (
            jnp.einsum("hqd,khd->hqk", grouped, keys, preferred_element_type=jnp.float32) * scale
        )
        probs = jnp.exp(jnp.where(allowed, scores - log_mass[:, :, None], far_below))
        probs_low = probs.astype(jnp.bfloat16)
        grad_values = jnp.einsum(
            "hqk,hqd->khd", probs_low, grad_grouped, preferred_element_type=jnp.float32
        )
        grad_probs = jnp.einsum(
            "hqd,khd->hqk", grad_grouped, values, preferred_element_type=jnp.float32
        )
        grad_scores = (probs * (grad_probs - delta[:, :, None]) * scale).astype(jnp.bfloat16)
        carried = carried + jnp.einsum(
            "hqk,khd->hqd", grad_scores, keys, preferred_element_type=jnp.float32
        )
        grad_keys = jnp.einsum(
            "hqk,hqd->khd", grad_scores, grouped, preferred_element_type=jnp.float32
        )
        joined = jnp.concatenate(
            [
                grad_keys.reshape(backward_size, kv_width),
                grad_values.reshape(backward_size, kv_width),
            ],
            axis=1,
        )
        return (carried, joined)

    grad_query_acc, block_grads = lax.scan(
        backward_one_block, grad_query_acc, (blocks_kv, blocks_at)
    )
    key_grads = block_grads.reshape(count, 2 * kv_width)
    grad_query_acc, all_key_grads = (grad_query_acc, key_grads)
    own_key_grads = lax.psum_scatter(
        all_key_grads, ("ctx", "fsdp"), scatter_dimension=0, tiled=True
    )
    grad_key = rotate(own_key_grads[:, :kv_width], own_places, KV_HEADS, -1.0).astype(jnp.bfloat16)
    grad_value = own_key_grads[:, kv_width:].astype(jnp.bfloat16)
    grad_query = rotate(from_groups(grad_query_acc, local_rows), own_places, HEADS, -1.0).astype(
        jnp.bfloat16
    )
    grad_query_w = jnp.einsum(
        "td,tq->dq", hidden_one, grad_query, preferred_element_type=jnp.float32
    )
    grad_key_w = jnp.einsum("td,tk->dk", hidden_one, grad_key, preferred_element_type=jnp.float32)
    grad_value_w = jnp.einsum(
        "td,tk->dk", hidden_one, grad_value, preferred_element_type=jnp.float32
    )
    grad_hidden_one = (
        jnp.einsum("tq,dq->td", grad_query, whole_query, preferred_element_type=jnp.float32)
        + jnp.einsum("tk,dk->td", grad_key, whole_key, preferred_element_type=jnp.float32)
        + jnp.einsum("tk,dk->td", grad_value, whole_value, preferred_element_type=jnp.float32)
    )
    grad_gain_one = jnp.sum(grad_hidden_one * normal_one, axis=0)
    grad_normal_one = grad_hidden_one * gain_one.astype(jnp.float32)[None, :]
    grad_tokens = (
        inverse_one
        * (
            grad_normal_one
            - normal_one * jnp.mean(grad_normal_one * normal_one, axis=1, keepdims=True)
        )
        + grad_resid
    )
    summed = (
        lax.psum(grad_gain_one.astype(jnp.bfloat16), "ctx").astype(jnp.float32),
        lax.psum(grad_gain_two.astype(jnp.bfloat16), "ctx").astype(jnp.float32),
        lax.psum(grad_query_w.astype(jnp.bfloat16), "ctx").astype(jnp.float32),
        lax.psum(grad_key_w.astype(jnp.bfloat16), "ctx").astype(jnp.float32),
        lax.psum(grad_value_w.astype(jnp.bfloat16), "ctx").astype(jnp.float32),
        lax.psum(grad_out_w.astype(jnp.bfloat16), "ctx").astype(jnp.float32),
        lax.psum(grad_gate_w.astype(jnp.bfloat16), "ctx").astype(jnp.float32),
        lax.psum(grad_up_w.astype(jnp.bfloat16), "ctx").astype(jnp.float32),
        lax.psum(grad_down.astype(jnp.bfloat16), "ctx").astype(jnp.float32),
    )
    shares = (
        lax.psum_scatter(
            summed[0].astype(jnp.bfloat16), "fsdp", scatter_dimension=0, tiled=True
        ).astype(jnp.float32),
        lax.psum_scatter(
            summed[1].astype(jnp.bfloat16), "fsdp", scatter_dimension=0, tiled=True
        ).astype(jnp.float32),
        lax.psum_scatter(
            summed[2].astype(jnp.bfloat16), "fsdp", scatter_dimension=0, tiled=True
        ).astype(jnp.float32),
        lax.psum_scatter(
            summed[3].astype(jnp.bfloat16), "fsdp", scatter_dimension=0, tiled=True
        ).astype(jnp.float32),
        lax.psum_scatter(
            summed[4].astype(jnp.bfloat16), "fsdp", scatter_dimension=0, tiled=True
        ).astype(jnp.float32),
        lax.psum_scatter(
            summed[5].astype(jnp.bfloat16), "fsdp", scatter_dimension=0, tiled=True
        ).astype(jnp.float32),
        lax.psum_scatter(
            summed[6].astype(jnp.bfloat16), "fsdp", scatter_dimension=0, tiled=True
        ).astype(jnp.float32),
        lax.psum_scatter(
            summed[7].astype(jnp.bfloat16), "fsdp", scatter_dimension=0, tiled=True
        ).astype(jnp.float32),
        lax.psum_scatter(
            summed[8].astype(jnp.bfloat16), "fsdp", scatter_dimension=0, tiled=True
        ).astype(jnp.float32),
    )
    return (
        layer_out,
        grad_tokens,
        shares[0],
        shares[1],
        shares[2],
        shares[3],
        shares[4],
        shares[5],
        shares[6],
        shares[7],
        shares[8],
    )


def solution(mesh):
    return jax.shard_map(
        body,
        mesh=mesh,
        in_specs=(
            P(("ctx", "fsdp"), None),
            P(),
            P("fsdp"),
            P("fsdp"),
            P("fsdp", None),
            P("fsdp", None),
            P("fsdp", None),
            P("fsdp", None),
            P("fsdp", None),
            P("fsdp", None),
            P("fsdp", None),
            P(("ctx", "fsdp"), None),
        ),
        out_specs=(
            P(("ctx", "fsdp"), None),
            P(("ctx", "fsdp"), None),
            P("fsdp"),
            P("fsdp"),
            P("fsdp", None),
            P("fsdp", None),
            P("fsdp", None),
            P("fsdp", None),
            P("fsdp", None),
            P("fsdp", None),
            P("fsdp", None),
        ),
        check_vma=False,
    )
```

profile of v0, /device:TPU:0, one launch (start us, length us, event | category | flops | bytes accessed | tf_op | source)
XLA Modules:
  0.0 1339.3 jit_solution(16399058916036183555)
XLA Ops:
  8.0 22.5 %all-gather.1 = bf16[4,240,320]{1,2,0:T(8,128)(2,1)S(1)} all-gather(bf16[1,240,320]{1,2,0:T(8,128)(2,1)} %bitcast.233), channel_id=1, replica_groups=mesh['ctx'=8,'fsdp'=4] {'fsdp'}, dimensions={0}, use_global_device_ids=true | all-gather | bytes 768000 | tf_op jit(solution)/shard_map/all_gather | solution.py:86
  33.4 11.6 all-reduce.7
  45.0 24.4 %all-gather = bf16[4,240,320]{1,2,0:T(8,128)(2,1)S(1)} all-gather(bf16[1,240,320]{1,2,0:T(8,128)(2,1)S(1)} %bitcast.234), channel_id=1, replica_groups=mesh['ctx'=8,'fsdp'=4] {'fsdp'}, dimensions={0}, use_global_device_ids=true | all-gather | bytes 768000 | tf_op jit(solution)/shard_map/all_gather | solution.py:85
  75.4 2.6 fusion.41
  78.2 66.1 %all-gather.9.cloned.1.call-done = bf16[4096,640]{0,1:T(8,128)(2,1)} async-done(((bf16[128,640]{0,1:T(8,128)(2,1)}), bf16[4096,640]{0,1:T(8,128)(2,1)}) %all-gather.9.cloned.1.call-update) | async-done | bytes 5242896 | tf_op jit(solution)/shard_map/all_gather | solution.py:126
  144.3 5.3 copy.101
  149.6 47.4 %while.28 = (s32[]{:T(128)}, f32[5,384,64]{1,2,0:T(8,128)S(1)}, f32[5,384]{1,0:T(8,128)S(1)}, f32[5,384]{1,0:T(8,128)S(1)}, s32[16,256]{1,0:T(8,128)S(1)}, /*ind...) while((s32[]{:T(128)}, f32[5,384,64]{1,2,0:T(8,128)S(1)}, ...), condition=%wide.region_4.5_spmd.clone, body=%wide.region_1.4_spmd.clone.sunk | while | flops 132695424 | bytes 9288321 | solution.py:152
  149.6 1.0 dynamic-slice_bitcast_fusion.4
  194.1 1.0 dynamic-slice_bitcast_fusion.4
  197.4 2.7 multiply_reduce_fusion.2
  200.3 80.3 %all-gather.15.cloned.1.call-done = bf16[960,2560]{1,0:T(8,128)(2,1)} async-done(((bf16[240,2560]{1,0:T(8,128)(2,1)}), bf16[960,2560]{1,0:T(8,128)(2,1)}) %all-gather.15.cloned.1.call-update) | async-done | bytes 4915216 | tf_op jit(solution)/shard_map/all_gather | solution.py:88
  280.6 4.3 fusion.51
  284.9 88.2 %all-gather.17.cloned.1.call-done = bf16[960,2560]{1,0:T(8,128)(2,1)} async-done(((bf16[240,2560]{1,0:T(8,128)(2,1)}), bf16[960,2560]{1,0:T(8,128)(2,1)}) %all-gather.17.cloned.1.call-update) | async-done | bytes 4915216 | tf_op jit(solution)/shard_map/all_gather | solution.py:89
  373.1 4.3 fusion.52
  377.5 88.2 %all-gather.19.cloned.1.call-done = bf16[2560,960]{0,1:T(8,128)(2,1)} async-done(((bf16[640,960]{0,1:T(8,128)(2,1)}), bf16[2560,960]{0,1:T(8,128)(2,1)}) %all-gather.19.cloned.1.call-update) | async-done | bytes 4915216 | tf_op jit(solution)/shard_map/all_gather | solution.py:90
  465.7 5.3 multiply_convert_fusion
  471.0 4.3 fusion.53
  475.4 1.6 multiply_reduce_fusion
  478.4 105.2 %while.29 = (s32[]{:T(128)}, f32[5,384,64]{1,2,0:T(8,128)}, f32[16,256,640]{2,1,0:T(8,128)}, s32[16,256]{1,0:T(8,128)S(1)}, bf16[16,256,640]{1,2,0:T(8,128)(2,1)...) while((s32[]{:T(128)}, f32[5,384,64]{1,2,0:T(8,128)}, ...), condition=%wide.region_9.10_spmd.clone, body=%wide.region_8.9_spmd.clone.sunk | while | flops 319012864 | bytes 18092720 | solution.py:238
  480.8 2.0 convolution_add_fusion.9
  487.2 2.2 convolution_add_fusion.9
  493.8 2.2 convolution_add_fusion.9
  500.3 2.2 convolution_add_fusion.9
  506.9 2.2 convolution_add_fusion.9
  513.5 2.2 convolution_add_fusion.9
  520.0 2.2 convolution_add_fusion.9
  526.6 2.2 convolution_add_fusion.9
  533.2 2.2 convolution_add_fusion.9
  539.8 2.2 convolution_add_fusion.9
  546.4 2.2 convolution_add_fusion.9
  553.0 2.2 convolution_add_fusion.9
  559.6 2.2 convolution_add_fusion.9
  566.2 2.2 convolution_add_fusion.9
  572.8 2.2 convolution_add_fusion.9
  579.4 2.2 convolution_add_fusion.9
  584.7 3.6 convolution_convert_fusion
  588.3 7.9 copy.82
  596.3 215.1 %reduce-scatter.15.cloned.1.call-done = f32[128,640]{1,0:T(8,128)} async-done(((f32[4096,640]{1,0:T(8,128)}), f32[128,640]{1,0:T(8,128)}) %reduce-scatter.15.cloned.1.call-update) | async-done | bytes 327696 | tf_op jit(solution)/shard_map/reduce_scatter | solution.py:243
  813.0 1.2 copy.78
  814.8 1.2 copy.80
  816.4 2.0 convolution_convert_fusion.4
  818.6 2.0 convolution_convert_fusion.3
  820.6 3.6 convolution_convert_fusion.2
  825.3 3.7 convolution_convert_fusion.1
  829.0 75.9 %reduce-scatter.29.cloned.1.call-done = bf16[640,960]{1,0:T(8,128)(2,1)} async-done(((bf16[2560,960]{1,0:T(8,128)(2,1)}), bf16[640,960]{1,0:T(8,128)(2,1)}) %reduce-scatter.29.cloned.1.call-update) | async-done | bytes 1228816
  904.9 2.4 copy.83
  907.3 23.9 %reduce-scatter.25.cloned.1.call-done = bf16[240,320]{1,0:T(8,128)(2,1)} async-done(((bf16[960,320]{1,0:T(8,128)(2,1)}), bf16[240,320]{1,0:T(8,128)(2,1)}) %reduce-scatter.25.cloned.1.call-update) | async-done | bytes 153616
  931.2 1.7 copy.79
  932.9 23.1 %reduce-scatter.27.cloned.1.call-done = bf16[240,320]{1,0:T(8,128)(2,1)} async-done(((bf16[960,320]{1,0:T(8,128)(2,1)}), bf16[240,320]{1,0:T(8,128)(2,1)}) %reduce-scatter.27.cloned.1.call-update) | async-done | bytes 153616
  956.0 1.7 copy.81
  957.7 41.9 %reduce-scatter.17.cloned.1.call-done = bf16[240,960]{1,0:T(8,128)(2,1)} async-done(((bf16[960,960]{1,0:T(8,128)(2,1)}), bf16[240,960]{1,0:T(8,128)(2,1)}) %reduce-scatter.17.cloned.1.call-update) | async-done | bytes 460816 | tf_op jit(solution)/shard_map/reduce_scatter | solution.py:291
  999.5 43.4 %reduce-scatter.19.cloned.1.call-done = bf16[240,960]{1,0:T(8,128)(2,1)} async-done(((bf16[960,960]{1,0:T(8,128)(2,1)}), bf16[240,960]{1,0:T(8,128)(2,1)}) %reduce-scatter.19.cloned.1.call-update) | async-done | bytes 460816 | tf_op jit(solution)/shard_map/reduce_scatter | solution.py:300
  1043.0 90.0 %reduce-scatter.21.cloned.1.call-done = bf16[240,2560]{1,0:T(8,128)(2,1)} async-done(((bf16[960,2560]{1,0:T(8,128)(2,1)}), bf16[240,2560]{1,0:T(8,128)(2,1)}) %reduce-scatter.21.cloned.1.call-update) | async-done | bytes 1228816 | tf_op jit(solution)/shard_map/reduce_scatter | solution.py:303
  1133.0 91.3 %reduce-scatter.23.cloned.1.call-done = bf16[240,2560]{1,0:T(8,128)(2,1)} async-done(((bf16[960,2560]{1,0:T(8,128)(2,1)}), bf16[240,2560]{1,0:T(8,128)(2,1)}) %reduce-scatter.23.cloned.1.call-update) | async-done | bytes 1228816 | tf_op jit(solution)/shard_map/reduce_scatter | solution.py:306
  1225.4 4.6 fusion.23
  1232.3 10.9 all-reduce.6
  1243.4 12.9 all-reduce.4
  1258.4 63.6 %all-reduce.10.cloned.1.call-done = (bf16[240,960]{1,0:T(8,128)(2,1)}, bf16[240,320]{0,1:T(8,128)(2,1)}, bf16[240,320]{0,1:T(8,128)(2,1)}, bf16[240,960]{1,0:T(8...) async-done(((bf16[240,960]{1,0:T(8,128)(2,1)}, bf16[240,320]{0,1:T(8,128)(2,1)}, bf16[240,320]{0,1:T(8,128)(2,1)}, ...) | async-done | bytes 4915216 | tf_op jit(solution)/shard_map/psum | solution.py:276
  1322.1 2.2 convert_element_type.177
  1324.3 1.7 convert_element_type.179
  1326.7 1.1 convert_element_type.183
  1327.7 1.7 convert_element_type.185
  1329.5 1.7 convert_element_type.187
  1331.2 1.6 convert_element_type.189
  (585 shorter events, 134.2 us)
Async XLA Ops:
  7.2 24.5 %copy-start.33 = (u32[32]{0:T(128)S(1)}, u32[32]{0:T(128)}, u32[]{:S(2)}) copy-start(u32[32]{0:T(128)} %constant.79) | copy-start | bytes 388
  7.2 25.7 %copy-start.34 = (bf16[240]{0:T(256)(128)(2,1)S(1)}, bf16[240]{0:T(256)(128)(2,1)}, u32[]{:S(2)}) copy-start(bf16[240]{0:T(256)(128)(2,1)} %param.18) | copy-start | bytes 1444
  7.2 25.9 %copy-start.35 = (bf16[240]{0:T(256)(128)(2,1)S(1)}, bf16[240]{0:T(256)(128)(2,1)}, u32[]{:S(2)}) copy-start(bf16[240]{0:T(256)(128)(2,1)} %param.19) | copy-start | bytes 1444
  7.2 37.8 %copy-start.31 = (bf16[240,320]{0,1:T(8,128)(2,1)S(1)}, bf16[240,320]{0,1:T(8,128)(2,1)}, u32[]{:S(2)}) copy-start(bf16[240,320]{0,1:T(8,128)(2,1)} %param.21) | copy-start | bytes 460804
  7.2 68.2 %all-gather.11.cloned.1.call-start = ((), (), s32[]{:S(2)}) async-start(), calls=%async_computation.9 | async-start | bytes 2457600 | tf_op jit(solution)/shard_map/all_gather | solution.py:84
  8.0 136.4 %all-gather.9.cloned.1.call-start = ((), (), s32[]{:S(2)}) async-start(), calls=%async_computation.8 | async-start | bytes 5406720 | tf_op jit(solution)/shard_map/all_gather | solution.py:126
  31.6 40.0 %copy-start.18 = (bf16[960,320]{0,1:T(8,128)(2,1)}, bf16[960,320]{0,1:T(8,128)(2,1)S(1)}, u32[]{:S(2)}) copy-start(bf16[960,320]{0,1:T(8,128)(2,1)S(1)} %reshape.280) | copy-start | bytes 1843204
  31.6 38.9 %copy-start.36 = (s32[32]{0:T(128)S(1)}, s32[32]{0:T(128)}, u32[]{:S(2)}) copy-start(s32[32]{0:T(128)} %param.17) | copy-start | bytes 388
  31.6 39.1 %copy-start.3 = (bf16[128,960]{0,1:T(8,128)(2,1)S(1)}, bf16[128,960]{0,1:T(8,128)(2,1)}, u32[]{:S(2)}) copy-start(bf16[128,960]{0,1:T(8,128)(2,1)} %param.16) | copy-start | bytes 737284
  70.4 3.0 copy-start.20
  72.7 124.7 %all-gather.13.cloned.1.call-start = ((), (), s32[]{:S(2)}) async-start(), calls=%async_computation.10 | async-start | bytes 2457600 | tf_op jit(solution)/shard_map/all_gather | solution.py:87
  73.5 207.1 %all-gather.15.cloned.1.call-start = ((), (), s32[]{:S(2)}) async-start(), calls=%async_computation.11 | async-start | bytes 6144000 | tf_op jit(solution)/shard_map/all_gather | solution.py:88
  74.0 299.1 %all-gather.17.cloned.1.call-start = ((), (), s32[]{:S(2)}) async-start(), calls=%async_computation.12 | async-start | bytes 6144000 | tf_op jit(solution)/shard_map/all_gather | solution.py:89
  74.6 391.1 %all-gather.19.cloned.1.call-start = ((), (), s32[]{:S(2)}) async-start(), calls=%async_computation.13 | async-start | bytes 6144000 | tf_op jit(solution)/shard_map/all_gather | solution.py:90
  75.2 736.2 %reduce-scatter.15.cloned.1.call-start = ((), (), s32[]{:S(2)}) async-start(), calls=%async_computation.14 | async-start | bytes 10813440 | tf_op jit(solution)/shard_map/reduce_scatter | solution.py:243
  197.4 2.7 copy-start.22
  200.1 276.9 %copy-start.5 = (f32[128,960]{0,1:T(8,128)}, f32[128,960]{0,1:T(8,128)S(1)}, u32[]{:S(2)}) copy-start(f32[128,960]{0,1:T(8,128)S(1)} %get-tuple-element.333) | copy-start | bytes 1474564
  200.3 172.8 %copy-start.7 = (bf16[128,960]{0,1:T(8,128)(2,1)}, bf16[128,960]{0,1:T(8,128)(2,1)S(1)}, u32[]{:S(2)}) copy-start(bf16[128,960]{0,1:T(8,128)(2,1)S(1)} %multiply_convert_fusion.3) | copy-start | bytes 737284
  284.9 180.8 %copy-start.24 = (bf16[128,960]{0,1:T(8,128)(2,1)S(1)}, bf16[128,960]{0,1:T(8,128)(2,1)}, u32[]{:S(2)}) copy-start(bf16[128,960]{0,1:T(8,128)(2,1)} %param.27) | copy-start | bytes 737284
  471.0 4.4 copy-start.14
  471.0 4.4 copy-start.16
  471.0 4.4 copy-start
  475.4 1.8 copy-start.10
  477.2 0.9 copy-start.11
  479.5 0.8 copy-start.2
  485.9 0.8 copy-start.2
  492.4 0.8 copy-start.2
  505.6 0.8 copy-start.2
  512.2 0.8 copy-start.2
  518.7 0.8 copy-start.2
  525.3 0.8 copy-start.2
  538.5 0.8 copy-start.2
  551.6 0.8 copy-start.2
  558.3 0.8 copy-start.2
  564.9 0.8 copy-start.2
  571.5 0.8 copy-start.2
  578.0 0.8 copy-start.2
  583.6 1.1 copy-start.13
  583.6 1.1 copy-start.25
  583.6 321.3 %reduce-scatter.29.cloned.1.call-start = ((), (), s32[]{:S(2)}) async-start(), calls=%async_computation.21 | async-start | bytes 6553600
  596.2 216.3 %copy-start.4 = (bf16[128,960]{0,1:T(8,128)(2,1)S(1)}, bf16[128,960]{0,1:T(8,128)(2,1)}, u32[]{:S(2)}) copy-start(bf16[128,960]{0,1:T(8,128)(2,1)} %param.16) | copy-start | bytes 737284
  596.2 335.0 %reduce-scatter.25.cloned.1.call-start = ((), (), s32[]{:S(2)}) async-start(), calls=%async_computation.19 | async-start | bytes 921600
  812.3 1.9 copy-start.29
  814.1 1.9 copy-start.1
  814.2 141.8 %reduce-scatter.27.cloned.1.call-start = ((), (), s32[]{:S(2)}) async-start(), calls=%async_computation.20 | async-start | bytes 921600
  816.0 183.5 %reduce-scatter.17.cloned.1.call-start = ((), (), s32[]{:S(2)}) async-start(), calls=%async_computation.15 | async-start | bytes 2457600 | tf_op jit(solution)/shard_map/reduce_scatter | solution.py:291
  816.4 2.1 copy-start.12
  816.4 2.1 copy-start.23
  818.5 2.1 copy-start.8
  818.5 2.1 copy-start.15
  818.5 224.5 %reduce-scatter.19.cloned.1.call-start = ((), (), s32[]{:S(2)}) async-start(), calls=%async_computation.16 | async-start | bytes 2457600 | tf_op jit(solution)/shard_map/reduce_scatter | solution.py:300
  820.5 312.5 %reduce-scatter.21.cloned.1.call-start = ((), (), s32[]{:S(2)}) async-start(), calls=%async_computation.17 | async-start | bytes 6144000 | tf_op jit(solution)/shard_map/reduce_scatter | solution.py:303
  824.2 1.1 copy-start.17
  824.2 400.1 %reduce-scatter.23.cloned.1.call-start = ((), (), s32[]{:S(2)}) async-start(), calls=%async_computation.18 | async-start | bytes 6144000 | tf_op jit(solution)/shard_map/reduce_scatter | solution.py:306
  829.0 493.1 %all-reduce.10.cloned.1.call-start = ((), (), s32[]{:S(2)}) async-start(), calls=%async_computation.22 | async-start | bytes 9994240 | tf_op jit(solution)/shard_map/psum | solution.py:276
  1224.3 1.0 copy-start.6
  1225.3 4.6 copy-start.21
  1225.3 5.1 copy-start.19
  1230.0 1.5 copy-start.9
  1322.0 3.9 copy-start.32
  1322.0 4.6 copy-start.30
  1322.0 5.7 copy-start.28
  1327.7 1.7 copy-start.27
  1329.5 1.7 copy-start.26
  (3 other events, 2.5 us)
Sparse Core Ops, SparseCore 0:
  9.6 59.2 all-gather.10
  72.8 71.4 all-gather.8
  145.9 41.7 all-gather.12
  189.1 91.4 all-gather.14
  282.0 91.0 all-gather.16
  374.6 91.0 all-gather.18
  583.7 227.5 reduce-scatter.14
  813.7 91.1 reduce-scatter.28
  907.8 23.3 reduce-scatter.24
  933.9 22.0 reduce-scatter.26
  958.9 40.6 reduce-scatter.16
  1002.3 40.6 reduce-scatter.18
  1045.3 87.6 reduce-scatter.20
  1135.3 88.9 reduce-scatter.22
  1229.6 92.4 all-reduce.9
where the time goes:
time: 1340 us
  waiting for transfers between devices  994 us (74%)
  matrix products  134 us (10%)
  blocking collectives  82.3 us (6%)
  local copies, waits for them, and re-layouts  80.9 us (6%)
  other arithmetic  27.6 us (2%)
  between operations  16 us (1%)
    reduce_scatter x1, waiting for transfers between devices, body(): lax.psum_scatter(all_key_grads, ('ctx', 'fsdp'), scatter_dimension=0, til...  215 us
    unnamed x18, waiting for transfers between devices  126 us
    reduce_scatter x1, waiting for transfers between devices, body(): lax.psum_scatter(summed[7].astype(jnp.bfloat16), 'fsdp', scatter_dimensio...  91.3 us
    reduce_scatter x1, waiting for transfers between devices, body(): lax.psum_scatter(summed[6].astype(jnp.bfloat16), 'fsdp', scatter_dimensio...  90 us
    all_gather x1, waiting for transfers between devices, body(): lax.all_gather(w_down, 'fsdp', axis=0, tiled=True)  88.2 us
    all_gather x1, waiting for transfers between devices, body(): lax.all_gather(w_up, 'fsdp', axis=0, tiled=True)  88.2 us
    all_gather x1, waiting for transfers between devices, body(): lax.all_gather(w_gate, 'fsdp', axis=0, tiled=True)  80.3 us
    all_gather x1, waiting for transfers between devices, body(): gathered_kv = lax.all_gather(packed, ('ctx', 'fsdp'), axis=0, tiled=True)  66.1 us
  transfers between devices with their start and end apart: 15, of which 13 were waited for; matrix products, arithmetic and copies ran while one was open for 8% of the time, Pallas kernels for 0%

commit v1 on v0

v1 whole, which is shorter than its diff:
```python
import functools

import jax
import jax.numpy as jnp
from jax import lax
from jax.experimental import pallas as pl
from jax.experimental.pallas import tpu as pltpu
from jax.sharding import PartitionSpec as P

HEADS = 15
KV_HEADS = 5
HEAD = 64
TP = 8
GROUP = HEADS // KV_HEADS
epsilon = 1e-05
base_theta = 100000.0
far_below = -1e30
f32 = jnp.float32
bf16 = jnp.bfloat16
AXES = ("ctx", "fsdp")


def exchange(array, mask, count):
    return lax.ppermute(array, AXES, [(i, i ^ mask) for i in range(count)])


def nn(left, right):
    return lax.dot_general(left, right, (((1,), (0,)), ((), ())), preferred_element_type=f32)


def tn(left, right):
    return lax.dot_general(left, right, (((0,), (0,)), ((), ())), preferred_element_type=f32)


def nt(left, right):
    return lax.dot_general(left, right, (((1,), (1,)), ((), ())), preferred_element_type=f32)


def query_positions(base_ref, at, width, half_rows):
    lane = lax.broadcasted_iota(jnp.int32, (1, width), 1)
    place = jnp.zeros((1, width), jnp.int32)
    for block in range(width // half_rows):
        start = base_ref[at + block] - block * half_rows
        place = jnp.where(lane >= block * half_rows, start + lane, place)
    return place


def key_positions(base_ref, row, at, count, half_rows, width):
    offset = lax.broadcasted_iota(jnp.int32, (half_rows, width), 0)
    return jnp.concatenate([offset + base_ref[row, at + b] for b in range(count)], axis=0)


def attention_forward(groups, rows, half_rows):
    half = rows // 2
    blocks = half // half_rows
    wide = 256

    def kernel(sel_ref, key_base, query_base, q_ref, kv_ref, out_ref, lse_ref, kvt_ref, pos_ref):
        def turn(at, unused):
            which, group = at // groups, at % groups
            kvt_ref[which, group] = kv_ref[which, group].T
            return unused

        lax.fori_loop(0, 2 * groups, turn, 0)

        def place(at, unused):
            which, group = at // groups, at % groups
            for side in range(2):
                pos_ref[which, group, pl.ds(side * half, half), :] = key_positions(
                    key_base, at, side * blocks, blocks, half_rows, 128
                )
            return unused

        lax.fori_loop(0, 2 * groups, place, 0)
        for head in range(2):
            which = sel_ref[head]
            for q_side in range(2):
                for tile in range(half // wide):
                    lanes = q_side * half + tile * wide
                    places = query_positions(query_base, lanes // half_rows, wide, half_rows)
                    turned = q_ref[pl.ds(head * HEAD, HEAD), pl.ds(lanes, wide)]
                    padded = jnp.concatenate([turned, jnp.zeros_like(turned)], axis=0)

                    def step(k_side, masked, group, carry):
                        highest, mass, accum = carry
                        block = kv_ref[which, group, pl.ds(k_side * half, half), :]
                        scores = nn(block, padded)
                        if masked:
                            at = pos_ref[which, group, pl.ds(k_side * half, half), :]
                            at = jnp.concatenate([at] * (wide // 128), axis=1)
                            scores = jnp.where(at <= places, scores, far_below)
                        top = jnp.maximum(highest, jnp.max(scores, axis=0, keepdims=True))
                        weights = jnp.exp(scores - top)
                        fade = jnp.exp(highest - top)
                        mass = mass * fade + jnp.sum(weights, axis=0, keepdims=True)
                        values = kvt_ref[which, group, pl.ds(HEAD, HEAD), pl.ds(k_side * half, half)]
                        accum = accum * fade + nn(values, weights.astype(bf16))
                        return (top, mass, accum)

                    carry = (
                        jnp.full((1, wide), far_below, f32),
                        jnp.zeros((1, wide), f32),
                        jnp.zeros((HEAD, wide), f32),
                    )
                    carry = lax.fori_loop(
                        0, groups, functools.partial(step, 0, q_side == 0), carry
                    )
                    if q_side == 1:
                        carry = lax.fori_loop(0, groups, functools.partial(step, 1, True), carry)
                    highest, mass, accum = carry
                    out_ref[pl.ds(head * HEAD, HEAD), pl.ds(lanes, wide)] = accum / mass
                    lse_ref[pl.ds(head, 1), pl.ds(lanes, wide)] = highest + jnp.log(mass)

    smem = pl.BlockSpec(memory_space=pltpu.SMEM)
    vmem = pl.BlockSpec(memory_space=pltpu.VMEM)
    return pl.pallas_call(
        kernel,
        out_shape=(
            jax.ShapeDtypeStruct((2 * HEAD, rows), f32),
            jax.ShapeDtypeStruct((2, rows), f32),
        ),
        in_specs=[smem, smem, smem, vmem, vmem],
        out_specs=(vmem, vmem),
        scratch_shapes=[
            pltpu.VMEM((2, groups, 2 * HEAD, rows), bf16),
            pltpu.VMEM((2, groups, rows, 128), jnp.int32),
        ],
        compiler_params=pltpu.CompilerParams(vmem_limit_bytes=48 * 1024 * 1024),
        cost_estimate=pl.CostEstimate(
            flops=6 * rows * rows * groups * HEAD, bytes_accessed=4 * rows * 512, transcendentals=0
        ),
    )


def attention_backward(groups, rows, half_rows):
    half = rows // 2
    blocks = half // half_rows
    wide = 256

    def kernel(
        sel_ref, key_base, query_base, q_ref, kv_ref, g_ref, out_ref, lse_ref, dq_ref, dkv_ref,
        rq_ref, rg_ref, delta_ref, pos_ref,
    ):
        dkv_ref[...] = jnp.zeros_like(dkv_ref)
        dq_ref[...] = jnp.zeros_like(dq_ref)
        for head in range(2):
            own = pl.ds(head * HEAD, HEAD)
            turned = q_ref[own, :].T
            rq_ref[head] = jnp.concatenate([turned, jnp.zeros_like(turned)], axis=1)
            grad = g_ref[own, :]
            turned = grad.T
            rg_ref[head] = jnp.concatenate([jnp.zeros_like(turned), turned], axis=1)
            delta_ref[pl.ds(head, 1), :] = jnp.sum(
                grad.astype(f32) * out_ref[own, :], axis=0, keepdims=True
            )

        def one_group(group, unused):
            for head in range(2):
                which = sel_ref[head]
                own = pl.ds(head * HEAD, HEAD)
                for k_side in range(2):
                    keys_at = pl.ds(k_side * half, half)
                    block = kv_ref[which, group, keys_at, :]
                    turned_keys = block.T[:HEAD]
                    pos_ref[...] = key_positions(
                        key_base, which * groups + group, k_side * blocks, blocks, half_rows, 128
                    )
                    for q_side in range(k_side, 2):
                        for tile in range(half // wide):
                            lanes = pl.ds(q_side * half + tile * wide, wide)
                            turned = q_ref[own, lanes]
                            padded = jnp.concatenate([turned, jnp.zeros_like(turned)], axis=0)
                            scores = nn(block, padded)
                            if q_side == k_side:
                                places = query_positions(
                                    query_base,
                                    (q_side * half + tile * wide) // half_rows,
                                    wide,
                                    half_rows,
                                )
                                at = jnp.concatenate([pos_ref[...]] * (wide // 128), axis=1)
                                scores = jnp.where(at <= places, scores, far_below)
                            probs = jnp.exp(scores - lse_ref[pl.ds(head, 1), lanes])
                            grads = g_ref[own, lanes]
                            padded = jnp.concatenate([jnp.zeros_like(grads), grads], axis=0)
                            grad_probs = nn(block, padded)
                            grad_scores = probs * (grad_probs - delta_ref[pl.ds(head, 1), lanes])
                            probs = probs.astype(bf16)
                            grad_scores = grad_scores.astype(bf16)
                            dkv_ref[which, group, keys_at, :] += nn(
                                grad_scores, rq_ref[head, lanes, :]
                            ) + nn(probs, rg_ref[head, lanes, :])
                            dq_ref[own, lanes] += nn(turned_keys, grad_scores)
            return unused

        lax.fori_loop(0, groups, one_group, 0)

    smem = pl.BlockSpec(memory_space=pltpu.SMEM)
    vmem = pl.BlockSpec(memory_space=pltpu.VMEM)
    return pl.pallas_call(
        kernel,
        out_shape=(
            jax.ShapeDtypeStruct((2 * HEAD, rows), f32),
            jax.ShapeDtypeStruct((2, groups, rows, 2 * HEAD), f32),
        ),
        in_specs=[smem, smem, smem, vmem, vmem, vmem, vmem, vmem],
        out_specs=(vmem, vmem),
        scratch_shapes=[
            pltpu.VMEM((2, rows, 2 * HEAD), bf16),
            pltpu.VMEM((2, rows, 2 * HEAD), bf16),
            pltpu.VMEM((2, rows), f32),
            pltpu.VMEM((half, 128), jnp.int32),
        ],
        compiler_params=pltpu.CompilerParams(vmem_limit_bytes=56 * 1024 * 1024),
        cost_estimate=pl.CostEstimate(
            flops=15 * rows * rows * groups * HEAD, bytes_accessed=4 * rows * 512, transcendentals=0
        ),
    )


def half_swap(matrix):
    rows, width = matrix.shape
    split = matrix.reshape(rows, width // HEAD, 2, HEAD // 2)
    return jnp.flip(split, axis=2).reshape(rows, width)


def body(
    tokens,
    pair_order,
    gain_attn,
    gain_mlp,
    w_query,
    w_key,
    w_value,
    w_out,
    w_gate,
    w_up,
    w_down,
    cotangent,
):
    local_rows, width = tokens.shape
    half_rows = local_rows // 2
    nz = lax.axis_size("fsdp")
    outer = lax.axis_size("ctx") // TP
    count = lax.axis_size(AXES)
    groups = outer * nz
    rows = TP * local_rows
    half = rows // 2
    d_rows = w_query.shape[0]
    me = lax.axis_index(AXES)
    z = lax.axis_index("fsdp")
    tp = lax.axis_index("ctx") % TP
    send = functools.partial(exchange, count=count)
    group_mask = [(g // nz) * TP * nz + g % nz for g in range(groups)]

    def plane_gather(block):
        even = [block] + [send(block, j * nz) for j in range(2, TP, 2)]
        odd = [send(e, nz) for e in even]
        return [piece for pair in zip(even, odd) for piece in pair]

    def plane_scatter(blocks):
        kept = [
            blocks[j].astype(f32) + send(blocks[j + 1].astype(bf16), nz).astype(f32)
            for j in range(0, TP, 2)
        ]
        total = kept[0]
        for j in range(1, TP // 2):
            total = total + send(kept[j].astype(bf16), 2 * j * nz).astype(f32)
        return total

    def plane_trade(blocks):
        crossed = [send(blocks[j + 1], nz) for j in range(0, TP, 2)]
        result = []
        for j in range(0, TP, 2):
            pair = jnp.stack([blocks[j], crossed[j // 2]])
            if j > 0:
                pair = send(pair, j * nz)
            result += [pair[0], pair[1]]
        return result

    def from_z(block):
        slots = jnp.stack([block] + [send(block, s) for s in range(1, nz)])
        return [lax.dynamic_index_in_dim(slots, z ^ s, 0, keepdims=False) for s in range(nz)]

    def to_z(stacked):
        total = lax.dynamic_index_in_dim(stacked, z, 0, keepdims=False).astype(f32)
        for s in range(1, nz):
            piece = lax.dynamic_index_in_dim(stacked, z ^ s, 0, keepdims=False).astype(bf16)
            total = total + send(piece, s).astype(f32)
        step = 1
        while step < outer:
            total = total + send(total.astype(bf16), step * TP * nz).astype(f32)
            step *= 2
        return total

    def by_device(slots):
        stacked = jnp.stack(slots)
        return [lax.dynamic_index_in_dim(stacked, tp ^ j, 0, keepdims=False) for j in range(TP)]

    def in_halves(slots):
        shaped = jnp.stack(slots).reshape(TP, 2, half_rows, slots[0].shape[1])
        return shaped.transpose(1, 0, 2, 3).reshape(rows, slots[0].shape[1])

    def to_slots(matrix):
        shaped = matrix.reshape(2, TP, half_rows, matrix.shape[1])
        return [shaped[:, j].reshape(local_rows, matrix.shape[1]) for j in range(TP)]

    kv_index = (4 * (tp // 2)) // GROUP + tp % 2
    own_heads = 2 * HEAD
    w_q_own = lax.dynamic_slice_in_dim(
        jnp.pad(w_query, ((0, 0), (0, TP * own_heads - HEADS * HEAD))), tp * own_heads, own_heads, 1
    )
    pad_kv = ((0, 0), (0, HEAD))
    w_k_own = lax.dynamic_slice_in_dim(jnp.pad(w_key, pad_kv), kv_index * HEAD, HEAD, 1)
    w_v_own = lax.dynamic_slice_in_dim(jnp.pad(w_value, pad_kv), kv_index * HEAD, HEAD, 1)
    gains = jnp.zeros((16, 2 * own_heads), bf16)
    gains = gains.at[0, :d_rows].set(gain_attn).at[1, :d_rows].set(gain_mlp)
    first = jnp.concatenate([jnp.concatenate([w_q_own, w_k_own, w_v_own], axis=1), gains], axis=0)
    first = from_z(first)
    w_qkv = jnp.concatenate([f[:d_rows] for f in first], axis=0)
    gain_one = jnp.concatenate([f[d_rows, :d_rows] for f in first]).astype(f32)[None, :]
    gain_two = jnp.concatenate([f[d_rows + 1, :d_rows] for f in first]).astype(f32)[None, :]

    gathered = in_halves(plane_gather(tokens))
    last_block = 2 * count - 1
    slot_of = jnp.array(
        [[m | (j * nz) for j in range(TP)] for m in group_mask], dtype=jnp.int32
    )
    low = pair_order[me ^ slot_of]
    base = jnp.stack([low, last_block - low], axis=1) * half_rows
    query_base = base[0].reshape(2 * TP)
    partner = jnp.array([j ^ 1 for j in range(TP)], dtype=jnp.int32)
    key_base = jnp.stack([base, base[:, :, partner]]).reshape(2 * groups, 2 * TP)
    places = (query_base[:, None] + jnp.arange(half_rows, dtype=jnp.int32)[None, :]).reshape(-1)
    lane = jnp.arange(HEAD) % (HEAD // 2)
    freqs = base_theta ** (-2.0 * lane.astype(f32) / HEAD)
    angles = places.astype(f32)[:, None] * freqs[None, :]
    cosine = jnp.cos(angles)
    sine = jnp.sin(angles) * jnp.where(jnp.arange(HEAD) < HEAD // 2, -1.0, 1.0)[None, :]
    ones = jnp.ones_like(cosine)
    cosine = jnp.concatenate([cosine, cosine, cosine, ones], axis=1)
    sine = jnp.concatenate([sine, sine, sine, 0.0 * ones], axis=1)
    head_of = 2 * tp + jnp.arange(2)
    kv_of = head_of // GROUP
    select = jnp.where(kv_of == kv_index, 0, 1).astype(jnp.int32)

    inputs = gathered.astype(f32)
    inverse_one = lax.rsqrt(jnp.mean(inputs * inputs, axis=1, keepdims=True) + epsilon)
    normal_one = inputs * inverse_one
    hidden_one = (normal_one * gain_one).astype(bf16)
    qkv = nn(hidden_one, w_qkv)
    qkv = qkv * cosine + half_swap(qkv) * sine
    query_turned = (qkv[:, :own_heads].astype(bf16) * jnp.asarray(HEAD**-0.5, bf16)).T
    own_kv = qkv[:, own_heads:].astype(bf16)
    kv_slots = [own_kv] + [send(own_kv, m) for m in group_mask[1:]]
    kv_other = [send(slot, nz) for slot in kv_slots]
    kv_all = jnp.stack([jnp.stack(kv_slots), jnp.stack(kv_other)])

    w_out_own = lax.dynamic_slice_in_dim(
        jnp.pad(w_out, ((0, 0), (0, TP * own_heads - width))), tp * own_heads, own_heads, 1
    )
    w_out_cols = jnp.concatenate(from_z(w_out_own), axis=0)
    w_out_all = jnp.concatenate(by_device(plane_gather(w_out_cols)), axis=1)[:, :width]
    ff_z = w_down.shape[0]
    ff_part = ff_z // TP
    ff_own = ff_part * nz

    def ff_columns(matrix):
        shaped = matrix.reshape(d_rows, nz, ff_z)
        return lax.dynamic_slice_in_dim(shaped, tp * ff_part, ff_part, 2).reshape(d_rows, ff_own)

    w_gu = jnp.concatenate(
        from_z(jnp.concatenate([ff_columns(w_gate), ff_columns(w_up)], axis=1)), axis=0
    )
    w_dn = jnp.concatenate(
        from_z(lax.dynamic_slice_in_dim(w_down, tp * ff_part, ff_part, 0)), axis=0
    )
    cot = in_halves(plane_gather(cotangent))

    attended_turned, log_mass = attention_forward(groups, rows, half_rows)(
        select, key_base, query_base, query_turned, kv_all
    )
    attended_own = attended_turned.T.astype(bf16)

    def reorder(matrix, j):
        shaped = matrix.reshape(2, TP, half_rows, matrix.shape[1])
        picked = jnp.stack([shaped[:, k ^ j] for k in range(TP)], axis=1)
        return picked.reshape(matrix.shape)

    attended_slots = plane_gather(attended_own)
    attended_slots = [reorder(slot, j) for j, slot in enumerate(attended_slots)]
    attended_low = jnp.concatenate(by_device(attended_slots), axis=1)[:, :width]

    resid = inputs + nn(attended_low, w_out_all)
    inverse_two = lax.rsqrt(jnp.mean(resid * resid, axis=1, keepdims=True) + epsilon)
    normal_two = resid * inverse_two
    hidden_two = (normal_two * gain_two).astype(bf16)
    gate_up = nn(hidden_two, w_gu)
    gate, up_part = gate_up[:, :ff_own], gate_up[:, ff_own:]
    sigmoid_gate = jax.nn.sigmoid(gate)
    activated = gate * sigmoid_gate
    product = (activated * up_part).astype(bf16)
    grad_product = nt(cot, w_dn)
    grad_gate = grad_product * up_part * sigmoid_gate * (1.0 + gate * (1.0 - sigmoid_gate))
    grad_up = grad_product * activated
    grad_gu = jnp.concatenate([grad_gate.astype(bf16), grad_up.astype(bf16)], axis=1)
    partial_hidden = nt(grad_gu, w_gu)
    grad_gain_two = jnp.sum(partial_hidden * normal_two, axis=0)
    grad_hidden = plane_scatter(to_slots(partial_hidden))

    def own_rows(matrix):
        return jnp.concatenate([matrix[:half_rows], matrix[half : half + half_rows]], axis=0)

    own_resid, own_normal, own_inverse = (own_rows(m) for m in (resid, normal_two, inverse_two))
    grad_normal = grad_hidden * gain_two
    grad_resid = own_inverse * (
        grad_normal - own_normal * jnp.mean(grad_normal * own_normal, axis=1, keepdims=True)
    ) + cotangent.astype(f32)
    grad_branch = grad_resid.astype(bf16)
    grad_attended = nt(grad_branch, w_out_all).astype(bf16)

    def column_blocks(matrix):
        padded = jnp.pad(matrix, ((0, 0), (0, TP * own_heads - width)))
        return [
            lax.dynamic_slice_in_dim(padded, (tp ^ j) * own_heads, own_heads, 1) for j in range(TP)
        ]

    traded = plane_trade(
        [
            jnp.concatenate([a, b], axis=1)
            for a, b in zip(column_blocks(grad_attended), column_blocks(grad_branch))
        ]
    )
    traded = in_halves(traded)
    grads_turned = traded[:, :own_heads].T
    grad_out_own = tn(attended_low, traded[:, own_heads:])

    grad_query, grad_kv = attention_backward(groups, rows, half_rows)(
        select,
        key_base,
        query_base,
        query_turned,
        kv_all,
        grads_turned,
        attended_turned,
        log_mass,
    )
    grad_kv = grad_kv[0] + send(grad_kv[1].astype(bf16), nz).astype(f32)
    total_kv = grad_kv[0]
    for g in range(1, groups):
        total_kv = total_kv + send(grad_kv[g].astype(bf16), group_mask[g]).astype(f32)
    grad_qkv = jnp.concatenate([grad_query.T * HEAD**-0.5, total_kv], axis=1)
    grad_qkv = (grad_qkv * cosine - half_swap(grad_qkv) * sine).astype(bf16)
    grad_qkv_own = tn(hidden_one, grad_qkv)
    partial_hidden = nt(grad_qkv, w_qkv)
    grad_gain_one = jnp.sum(partial_hidden * normal_one, axis=0)
    grad_hidden = plane_scatter(to_slots(partial_hidden))
    own_normal, own_inverse = own_rows(normal_one), own_rows(inverse_one)
    grad_normal = grad_hidden * gain_one
    grad_tokens = (
        own_inverse
        * (grad_normal - own_normal * jnp.mean(grad_normal * own_normal, axis=1, keepdims=True))
        + grad_resid
    )
    layer_out = (own_resid + plane_scatter(to_slots(nn(product, w_dn)))).astype(bf16)

    def finish(matrix):
        part = to_z(matrix.reshape(nz, matrix.shape[0] // nz, matrix.shape[1])).astype(bf16)
        return by_device(plane_gather(part))

    down_parts = finish(tn(product, cot))
    grad_w_down = jnp.concatenate(down_parts, axis=0).astype(f32)
    gu_parts = jnp.stack(finish(tn(hidden_two, grad_gu)))
    gu_parts = gu_parts.reshape(TP, d_rows, 2, nz, ff_part).transpose(2, 1, 3, 0, 4)
    gu_parts = gu_parts.reshape(2, d_rows, nz * ff_z).astype(f32)
    grad_w_out = jnp.concatenate(finish(grad_out_own), axis=1)[:, :width].astype(f32)
    gain_rows = jnp.stack([grad_gain_one, grad_gain_two]).reshape(2, nz, d_rows).transpose(1, 0, 2)
    gain_rows = jnp.pad(gain_rows, ((0, 0), (0, 14), (0, 2 * own_heads - d_rows)))
    last = jnp.concatenate([grad_qkv_own.reshape(nz, d_rows, 2 * own_heads), gain_rows], axis=1)
    last = finish(last.reshape(nz * (d_rows + 16), 2 * own_heads))
    grad_w_query = jnp.concatenate([p[:d_rows, :own_heads] for p in last], axis=1)[:, :width]
    pieces = [p[:d_rows, own_heads:].astype(f32) for p in last]
    pieces = [pieces[0], pieces[1] + pieces[2], pieces[3] + pieces[4], pieces[5], pieces[6]]
    grad_w_key = jnp.concatenate([p[:, :HEAD] for p in pieces], axis=1)
    grad_w_value = jnp.concatenate([p[:, HEAD:] for p in pieces], axis=1)
    grad_gains = sum(p[d_rows : d_rows + 2, :d_rows].astype(f32) for p in last)
    return (
        layer_out,
        grad_tokens,
        grad_gains[0],
        grad_gains[1],
        grad_w_query.astype(f32),
        grad_w_key,
        grad_w_value,
        grad_w_out,
        gu_parts[0],
        gu_parts[1],
        grad_w_down,
    )


def solution(mesh):
    return jax.shard_map(
        body,
        mesh=mesh,
        in_specs=(
            P(("ctx", "fsdp"), None),
            P(),
            P("fsdp"),
            P("fsdp"),
            P("fsdp", None),
            P("fsdp", None),
            P("fsdp", None),
            P("fsdp", None),
            P("fsdp", None),
            P("fsdp", None),
            P("fsdp", None),
            P(("ctx", "fsdp"), None),
        ),
        out_specs=(
            P(("ctx", "fsdp"), None),
            P(("ctx", "fsdp"), None),
            P("fsdp"),
            P("fsdp"),
            P("fsdp", None),
            P("fsdp", None),
            P("fsdp", None),
            P("fsdp", None),
            P("fsdp", None),
            P("fsdp", None),
            P("fsdp", None),
        ),
        check_vma=False,
    )
```

time: 1340 us -> 560 us (0.42)
  waiting for transfers between devices: 994 us -> 134 us
  matrix products: 134 us -> 25.2 us
  local copies, waits for them, and re-layouts: 80.9 us -> 189 us
  starting transfers between devices: 0.83 us -> 95.3 us
  blocking collectives: 82.3 us -> 0 us
  Pallas kernels: 0 us -> 49.1 us
  other arithmetic: 27.6 us -> 52.9 us
    reduce_scatter x5 -> x0, waiting for transfers between devices: 482 us -> none  [the longest x1 215 us: body(): lax.psum_scatter(all_key_grads, ('ctx', 'fsdp'), scatter_dimension=0, til...]
    all_gather x6 -> x0, waiting for transfers between devices: 323 us -> none  [the longest x1 88.2 us: body(): lax.all_gather(w_down, 'fsdp', axis=0, tiled=True)]
    ppermute x0 -> x119, waiting for transfers between devices: none -> 134 us  [exchange(): return lax.ppermute(array, AXES, [(i, i ^ mask) for i in range(count)])]
    unnamed x18 -> x0, waiting for transfers between devices: 126 us -> none
    dot_general x133 -> x12, matrix products: 134 us -> 25.2 us  [the longest x4 12.3 us: nt(): lax.dot_general(left, right, (((1,), (1,)), ((), ())), preferred_element_...]
    ppermute x0 -> x119, starting transfers between devices: none -> 95.3 us  [exchange(): return lax.ppermute(array, AXES, [(i, i ^ mask) for i in range(count)])]
    psum x1 -> x0, waiting for transfers between devices: 63.6 us -> none  [body(): lax.psum(grad_query_w.astype(jnp.bfloat16), 'ctx').astype(jnp.float32)]
    pallas_call x0 -> x2, Pallas kernels: none -> 49.1 us  [the longest x1 25.7 us: body(): attention_forward(groups, rows, half_rows)]
  transfers between devices with their start and end apart: 15 -> 119, of which waited for: 13 -> 36; matrix products, arithmetic and copies ran while one was open for 8% -> 34% of each run, Pallas kernels for 0% -> 4%
where the time goes in v1:
time: 560 us; the launch traced here: 549 us
  local copies, waits for them, and re-layouts  189 us (34%)
  waiting for transfers between devices  134 us (24%)
  starting transfers between devices  95.3 us (17%)
  other arithmetic  52.9 us (9%)
  Pallas kernels  49.1 us (9%)
  matrix products  25.2 us (4%)
    ppermute x119, waiting for transfers between devices, exchange(): return lax.ppermute(array, AXES, [(i, i ^ mask) for i in range(count)])  134 us
    ppermute x119, starting transfers between devices, exchange(): return lax.ppermute(array, AXES, [(i, i ^ mask) for i in range(count)])  95.3 us
    unnamed x340, local copies, waits for them, and re-layouts  69.2 us
    pallas_call x1, Pallas kernels, body(): attention_forward(groups, rows, half_rows)  25.7 us
    pallas_call x1, Pallas kernels, body(): attention_backward(groups, rows, half_rows)  23.4 us
    convert_element_type x12, local copies, waits for them, and re-layouts, plane_scatter(): blocks[j + 1].astype(bf16)  20.4 us
    dot_general x4, matrix products, nt(): lax.dot_general(left, right, (((1,), (1,)), ((), ())), preferred_element_...  12.3 us
  transfers between devices with their start and end apart: 119, of which 36 were waited for; matrix products, arithmetic and copies ran while one was open for 34% of the time, Pallas kernels for 4%

profile of v1, /device:TPU:0, one launch (start us, length us, event | category | flops | bytes accessed | tf_op | source)
XLA Modules:
  0.0 549.3 jit_solution(8436044395137810811)
XLA Ops:
  3.1 2.5 collective-permute-start.1
  7.0 3.6 collective-permute-start.26
  20.2 2.4 copy.393
  22.6 2.4 copy.392
  32.9 3.7 collective-permute-start.9
  39.1 2.4 collective-permute-done.9
  41.5 3.6 collective-permute-start.39
  45.0 11.3 %collective-permute-done.8 = bf16[256,256]{1,0:T(8,128)(2,1)S(1)} collective-permute-done((bf16[256,256]{1,0:T(8,128)(2,1)}, bf16[256,256]{1,0:T(8,128)(2,1)S(1)}, u32[]{:S(2)}, u32[]{:S(2)}) %collective-permute-start.8) | collective-permute-done | bytes 131104 | tf_op jit(solution)/shard_map/ppermute | solution.py:24
  58.0 3.9 collective-permute-start.36
  61.9 19.2 %collective-permute-done.38 = bf16[80,960]{0,1:T(8,128)(2,1)S(1)} collective-permute-done((bf16[80,960]{0,1:T(8,128)(2,1)}, bf16[80,960]{0,1:T(8,128)(2,1)S(1)}, u32[]{:S(2)}, u32[]{:S(2)}) %collective-permute-start.38) | collective-permute-done | bytes 153632 | tf_op jit(solution)/shard_map/ppermute | solution.py:24
  87.8 3.4 collective-permute-done.48
  96.6 4.2 collective-permute-done.34
  105.4 3.7 collective-permute-done.28
  110.1 2.6 collective-permute-start.30
  116.7 2.2 copy.365
  119.0 5.5 %copy.391 = f32[1024,960]{0,1:T(8,128)} copy(f32[1024,960]{1,0:T(8,128)} %bitcast.467) | data formatting | bytes 7864320 | tf_op jit(solution)/shard_map/convert_element_type | solution.py:347
  124.6 4.5 multiply_convert_fusion.1
  139.3 2.3 collective-permute-start.12
  146.6 3.3 copy.409
  150.5 2.2 fusion.78
  152.7 2.1 collective-permute-start.10
  158.0 5.9 %collective-permute-done.11 = bf16[1024,128]{1,0:T(8,128)(2,1)S(1)} collective-permute-done((bf16[1024,128]{1,0:T(8,128)(2,1)S(1)}, bf16[1024,128]{1,0:T(8,128)(2,1)S(1)}, u32[]{:S(2)}, u32[]{:S(2)}) %collective-permute-start.11) | collective-permute-done | bytes 262176 | tf_op jit(solution)/shard_map/ppermute | solution.py:24
  163.9 2.9 collective-permute-done.10
  168.7 25.7 %shard_map.221 = (f32[128,1024]{1,0:T(8,128)S(1)}, f32[2,1024]{1,0:T(2,128)S(1)}) custom-call(s32[2]{0:T(128)S(1)} %compare_select_fusion.3.sel_ref, s32[8,16]{1,0:T(8,128)S(1)} %reshape.485.key_base, s32[16]{0:T(128)S(1)} %reshape_squeeze.51.query_base, bf16[128,1024]{1,0:T(8,128)(2,1)S(1)} %copy.376.q_ref, bf16[2,4,1024,128]{3,2,1,0:T(8,128)(2,1)S(1)} %pad_maximum_fusion.kv_ref), custom_call_target="tpu_custom_call" | custom-call | flops 1610612736 | bytes 2097152 | tf_op jit(solution)/shard_map/pallas_call | solution.py:380
  200.7 4.9 collective-permute-done.18
  208.6 3.5 collective-permute-done.20
  234.3 2.3 multiply_reduce_fusion.2
  247.2 4.2 multiply_reduce_fusion
  251.4 5.2 copy.410
  256.7 3.0 fusion.76
  269.4 2.2 fusion.82
  277.4 2.5 collective-permute-start.109
  279.9 2.0 copy.402
  316.0 2.5 collective-permute-start.99
  321.0 4.1 collective-permute-done.101
  325.1 17.8 %collective-permute-done.100 = bf16[240,640]{0,1:T(8,128)(2,1)S(1)} collective-permute-done((bf16[240,640]{0,1:T(8,128)(2,1)S(1)}, bf16[240,640]{0,1:T(8,128)(2,1)S(1)}, u32[]{:S(2)}, u32[]{:S(2)}) %collective-permute-start.100) | collective-permute-done | bytes 307232 | tf_op jit(solution)/shard_map/ppermute | solution.py:24
  345.5 6.2 %collective-permute-done.115 = bf16[80,960]{1,0:T(8,128)(2,1)S(1)} collective-permute-done((bf16[80,960]{1,0:T(8,128)(2,1)S(1)}, bf16[80,960]{1,0:T(8,128)(2,1)S(1)}, u32[]{:S(2)}, u32[]{:S(2)}) %collective-permute-start.115) | collective-permute-done | bytes 153632 | tf_op jit(solution)/shard_map/ppermute | solution.py:24
  362.2 2.9 copy.453
  372.3 3.1 collective-permute-done.46
  376.6 3.1 collective-permute-done.44
  380.4 2.2 fusion.26
  393.2 3.3 collective-permute-done.63
  397.1 2.4 collective-permute-done.67
  399.6 2.2 fusion.4
  402.8 2.0 collective-permute-start.91
  404.7 2.5 collective-permute-start.89
  407.2 23.4 %shard_map.222 = (f32[128,1024]{1,0:T(8,128)}, f32[2,4,1024,128]{3,2,1,0:T(8,128)}) custom-call(s32[2]{0:T(128)} %copy-done.7, s32[8,16]{1,0:T(8,128)} %copy-done.5, s32[16]{0:T(128)} %copy-done.6, bf16[128,1024]{1,0:T(8,128)(2,1)} %copy-done.4, bf16[2,4,1024,128]{3,2,1,0:T(8,128)(2,1)} %copy-done.3, bf16[128,1024]{1,0:T(8,128)(2,1)} %bitcast.574, ...), custom_call_target="tpu_custom_call" | custom-call | flops 4026531840 | bytes 2097152 | tf_op jit(solution)/shard_map/pallas_call | solution.py:438
  440.4 2.0 collective-permute-start.97
  442.5 3.0 collective-permute-done.97
  446.1 2.2 collective-permute-done.98
  456.8 2.2 collective-permute-start.71
  459.1 2.2 collective-permute-start.69
  464.9 3.2 copy.451
  468.0 3.5 copy.447
  471.5 3.2 copy.452
  474.7 6.8 %collective-permute-done.70 = bf16[1024,128]{1,0:T(8,128)(2,1)S(1)} collective-permute-done((bf16[1024,128]{1,0:T(8,128)(2,1)S(1)}, bf16[1024,128]{1,0:T(8,128)(2,1)S(1)}, u32[]{:S(2)}, u32[]{:S(2)}) %collective-permute-start.70) | collective-permute-done | bytes 262176 | tf_op jit(solution)/shard_map/ppermute | solution.py:24
  485.3 2.5 copy.429
  487.8 5.6 %multiply_reduce_fusion.1 = (f32[960]{0:T(1024)S(1)}, f32[1024,960]{0,1:T(8,128)}) fusion(f32[1024,960]{0,1:T(8,128)} %get-tuple-element.123, bf16[240,256]{1,0:T(8,128)(2,1)S(1)} %copy-done.65, bf16[240,256]{1,0:T(8,128)(2,1)} %get-tuple-element.192, bf16[240,256]{1,0:T(8,128)(2,1)} %get-tuple-element.193, bf16[240,256]{1,0:T(8,128)(2,1)S(1)} %copy-done.63, ...), kind=kOutput, calls=%fused_computation.7 | convolution fusion | flops 510131264 | bytes 10983168 | tf_op jit(solution)/shard_map/dot_general | solution.py:36
  493.4 5.5 %copy.430 = f32[1024,960]{1,0:T(8,128)} copy(f32[1024,960]{0,1:T(8,128)} %get-tuple-element.266) | data formatting | bytes 7864320 | tf_op jit(solution)/shard_map/dot_general | solution.py:36
  498.9 2.5 convert.39
  508.1 2.2 collective-permute-start.81
  510.2 2.2 collective-permute-start.79
  531.2 2.0 collective-permute-start.78
  542.7 3.4 collective-permute-done.76
  (779 shorter events, 257.8 us)
Async XLA Ops:
  2.6 79.9 %collective-permute-start = (bf16[128,960]{1,0:T(8,128)(2,1)}, bf16[128,960]{1,0:T(8,128)(2,1)}, u32[]{:S(2)}, u32[]{:S(2)}) collective-permute-start(bf16[128,960]{1,0:T(8,128)(2,1)} %copy.360), channel_id=1, source_target_pairs={{0,4},{1,5},{2,6},{3,7},{4,0},{5,1},{6,2},{7,3},{8,12},{9,13},{10,... | collective-permute-start | bytes 737288 | tf_op jit(solution)/shard_map/ppermute | solution.py:24
  3.1 80.9 %collective-permute-start.1 = (bf16[128,960]{1,0:T(8,128)(2,1)}, bf16[128,960]{1,0:T(8,128)(2,1)}, u32[]{:S(2)}, u32[]{:S(2)}) collective-permute-start(bf16[128,960]{1,0:T(8,128)(2,1)} %copy.360), channel_id=1, source_target_pairs={{0,8},{1,9},{2,10},{3,11},{4,12},{5,13},{6,14},{7,15},{8,0},{9,1},... | collective-permute-start | bytes 737288 | tf_op jit(solution)/shard_map/ppermute | solution.py:24
  7.0 25.9 %collective-permute-start.26 = (bf16[240,128]{1,0:T(8,128)(2,1)}, bf16[240,128]{1,0:T(8,128)(2,1)}, u32[]{:S(2)}, u32[]{:S(2)}) collective-permute-start(bf16[240,128]{1,0:T(8,128)(2,1)} %pad_dynamic-slice_fusion), channel_id=1, source_target_pairs={{0,3},{1,2},{2,1},{3,0},{4,7},{5,6},{6,5},{7,4},{8,11},{9,10},{10,... | collective-permute-start | bytes 184328 | tf_op jit(solution)/shard_map/ppermute | solution.py:24
  10.6 26.0 %collective-permute-start.25 = (bf16[240,128]{1,0:T(8,128)(2,1)}, bf16[240,128]{1,0:T(8,128)(2,1)}, u32[]{:S(2)}, u32[]{:S(2)}) collective-permute-start(bf16[240,128]{1,0:T(8,128)(2,1)} %pad_dynamic-slice_fusion), channel_id=1, source_target_pairs={{0,2},{1,3},{2,0},{3,1},{4,6},{5,7},{6,4},{7,5},{8,10},{9,11},{10,... | collective-permute-start | bytes 184328 | tf_op jit(solution)/shard_map/ppermute | solution.py:24
  10.6 26.0 %collective-permute-start.24 = (bf16[240,128]{1,0:T(8,128)(2,1)}, bf16[240,128]{1,0:T(8,128)(2,1)}, u32[]{:S(2)}, u32[]{:S(2)}) collective-permute-start(bf16[240,128]{1,0:T(8,128)(2,1)} %pad_dynamic-slice_fusion), channel_id=1, source_target_pairs={{0,1},{1,0},{2,3},{3,2},{4,5},{5,4},{6,7},{7,6},{8,9},{9,8},{10,11... | collective-permute-start | bytes 184328 | tf_op jit(solution)/shard_map/ppermute | solution.py:24
  36.6 19.7 %collective-permute-start.8 = (bf16[256,256]{1,0:T(8,128)(2,1)}, bf16[256,256]{1,0:T(8,128)(2,1)S(1)}, u32[]{:S(2)}, u32[]{:S(2)}) collective-permute-start(bf16[256,256]{1,0:T(8,128)(2,1)} %pad_maximum_fusion.21), channel_id=1, source_target_pairs={{0,2},{1,3},{2,0},{3,1},{4,6},{5,7},{6,4},{7,5},{8,10},{9,11},{10,... | collective-permute-start | bytes 393224 | tf_op jit(solution)/shard_map/ppermute | solution.py:24
  36.6 19.7 %collective-permute-start.7 = (bf16[256,256]{1,0:T(8,128)(2,1)}, bf16[256,256]{1,0:T(8,128)(2,1)S(1)}, u32[]{:S(2)}, u32[]{:S(2)}) collective-permute-start(bf16[256,256]{1,0:T(8,128)(2,1)} %pad_maximum_fusion.21), channel_id=1, source_target_pairs={{0,1},{1,0},{2,3},{3,2},{4,5},{5,4},{6,7},{7,6},{8,9},{9,8},{10,11... | collective-permute-start | bytes 393224 | tf_op jit(solution)/shard_map/ppermute | solution.py:24
  41.5 16.6 %collective-permute-start.39 = (bf16[80,960]{0,1:T(8,128)(2,1)}, bf16[80,960]{0,1:T(8,128)(2,1)S(1)}, u32[]{:S(2)}, u32[]{:S(2)}) collective-permute-start(bf16[80,960]{0,1:T(8,128)(2,1)} %constant_dynamic-slice_fusion.4), channel_id=1, source_target_pairs={{0,3},{1,2},{2,1},{3,0},{4,7},{5,6},{6,5},{7,4},{8,11},{9,10},{10,... | collective-permute-start | bytes 460808 | tf_op jit(solution)/shard_map/ppermute | solution.py:24
  56.3 24.7 %collective-permute-start.38 = (bf16[80,960]{0,1:T(8,128)(2,1)}, bf16[80,960]{0,1:T(8,128)(2,1)S(1)}, u32[]{:S(2)}, u32[]{:S(2)}) collective-permute-start(bf16[80,960]{0,1:T(8,128)(2,1)} %constant_dynamic-slice_fusion.4), channel_id=1, source_target_pairs={{0,2},{1,3},{2,0},{3,1},{4,6},{5,7},{6,4},{7,5},{8,10},{9,11},{10,... | collective-permute-start | bytes 460808 | tf_op jit(solution)/shard_map/ppermute | solution.py:24
  56.3 24.7 %collective-permute-start.37 = (bf16[80,960]{0,1:T(8,128)(2,1)}, bf16[80,960]{0,1:T(8,128)(2,1)S(1)}, u32[]{:S(2)}, u32[]{:S(2)}) collective-permute-start(bf16[80,960]{0,1:T(8,128)(2,1)} %constant_dynamic-slice_fusion.4), channel_id=1, source_target_pairs={{0,1},{1,0},{2,3},{3,2},{4,5},{5,4},{6,7},{7,6},{8,9},{9,8},{10,11... | collective-permute-start | bytes 460808 | tf_op jit(solution)/shard_map/ppermute | solution.py:24
  58.0 36.4 %collective-permute-start.36 = (bf16[240,640]{0,1:T(8,128)(2,1)S(1)}, bf16[240,640]{0,1:T(8,128)(2,1)S(1)}, u32[]{:S(2)}, u32[]{:S(2)}) collective-permute-start(bf16[240,640]{0,1:T(8,128)(2,1)S(1)} %copy-done.80), channel_id=1, source_target_pairs={{0,3},{1,2},{2,1},{3,0},{4,7},{5,6},{6,5},{7,4},{8,11},{9,10},{10,... | collective-permute-start | bytes 921608 | tf_op jit(solution)/shard_map/ppermute | solution.py:24
  81.1 15.6 %collective-permute-start.35 = (bf16[240,640]{0,1:T(8,128)(2,1)S(1)}, bf16[240,640]{0,1:T(8,128)(2,1)S(1)}, u32[]{:S(2)}, u32[]{:S(2)}) collective-permute-start(bf16[240,640]{0,1:T(8,128)(2,1)S(1)} %copy-done.80), channel_id=1, source_target_pairs={{0,2},{1,3},{2,0},{3,1},{4,6},{5,7},{6,4},{7,5},{8,10},{9,11},{10,... | collective-permute-start | bytes 921608 | tf_op jit(solution)/shard_map/ppermute | solution.py:24
  84.0 16.9 %collective-permute-start.34 = (bf16[240,640]{0,1:T(8,128)(2,1)S(1)}, bf16[240,640]{0,1:T(8,128)(2,1)S(1)}, u32[]{:S(2)}, u32[]{:S(2)}) collective-permute-start(bf16[240,640]{0,1:T(8,128)(2,1)S(1)} %copy-done.80), channel_id=1, source_target_pairs={{0,1},{1,0},{2,3},{3,2},{4,5},{5,4},{6,7},{7,6},{8,9},{9,8},{10,11... | collective-permute-start | bytes 921608 | tf_op jit(solution)/shard_map/ppermute | solution.py:24
  85.5 18.1 %collective-permute-start.3 = (bf16[128,960]{1,0:T(8,128)(2,1)}, bf16[128,960]{1,0:T(8,128)(2,1)S(1)}, u32[]{:S(2)}, u32[]{:S(2)}) collective-permute-start(bf16[128,960]{1,0:T(8,128)(2,1)} %copy.360), channel_id=1, source_target_pairs={{0,16},{1,17},{2,18},{3,19},{4,20},{5,21},{6,22},{7,23},{8,24},{9,... | collective-permute-start | bytes 737288 | tf_op jit(solution)/shard_map/ppermute | solution.py:24
  91.3 18.8 %collective-permute-start.5 = (bf16[128,960]{1,0:T(8,128)(2,1)}, bf16[128,960]{1,0:T(8,128)(2,1)S(1)}, u32[]{:S(2)}, u32[]{:S(2)}) collective-permute-start(bf16[128,960]{1,0:T(8,128)(2,1)} %copy.360), channel_id=1, source_target_pairs={{0,24},{1,25},{2,26},{3,27},{4,28},{5,29},{6,30},{7,31},{8,16},{9,... | collective-permute-start | bytes 737288 | tf_op jit(solution)/shard_map/ppermute | solution.py:24
  94.4 19.9 %collective-permute-start.50 = (bf16[128,960]{1,0:T(8,128)(2,1)S(1)}, bf16[128,960]{1,0:T(8,128)(2,1)}, u32[]{:S(2)}, u32[]{:S(2)}) collective-permute-start(bf16[128,960]{1,0:T(8,128)(2,1)S(1)} %copy-done.49), channel_id=1, source_target_pairs={{0,16},{1,17},{2,18},{3,19},{4,20},{5,21},{6,22},{7,23},{8,24},{9,... | collective-permute-start | bytes 737288 | tf_op jit(solution)/shard_map/ppermute | solution.py:24
  103.7 11.5 %collective-permute-start.52 = (bf16[128,960]{1,0:T(8,128)(2,1)S(1)}, bf16[128,960]{1,0:T(8,128)(2,1)}, u32[]{:S(2)}, u32[]{:S(2)}) collective-permute-start(bf16[128,960]{1,0:T(8,128)(2,1)S(1)} %copy-done.49), channel_id=1, source_target_pairs={{0,24},{1,25},{2,26},{3,27},{4,28},{5,29},{6,30},{7,31},{8,16},{9,... | collective-permute-start | bytes 737288 | tf_op jit(solution)/shard_map/ppermute | solution.py:24
  110.1 24.9 %collective-permute-start.30 = (bf16[960,128]{1,0:T(8,128)(2,1)}, bf16[960,128]{1,0:T(8,128)(2,1)}, u32[]{:S(2)}, u32[]{:S(2)}) collective-permute-start(bf16[960,128]{1,0:T(8,128)(2,1)} %pad_maximum_fusion.18), channel_id=1, source_target_pairs={{0,16},{1,17},{2,18},{3,19},{4,20},{5,21},{6,22},{7,23},{8,24},{9,... | collective-permute-start | bytes 737288 | tf_op jit(solution)/shard_map/ppermute | solution.py:24
  113.0 22.1 %collective-permute-start.32 = (bf16[960,128]{1,0:T(8,128)(2,1)}, bf16[960,128]{1,0:T(8,128)(2,1)}, u32[]{:S(2)}, u32[]{:S(2)}) collective-permute-start(bf16[960,128]{1,0:T(8,128)(2,1)} %pad_maximum_fusion.18), channel_id=1, source_target_pairs={{0,24},{1,25},{2,26},{3,27},{4,28},{5,29},{6,30},{7,31},{8,16},{9,... | collective-permute-start | bytes 737288 | tf_op jit(solution)/shard_map/ppermute | solution.py:24
  114.3 21.3 %collective-permute-start.49 = (bf16[128,960]{1,0:T(8,128)(2,1)}, bf16[128,960]{1,0:T(8,128)(2,1)}, u32[]{:S(2)}, u32[]{:S(2)}) collective-permute-start(bf16[128,960]{1,0:T(8,128)(2,1)} %collective-permute-done.48), channel_id=1, source_target_pairs={{0,4},{1,5},{2,6},{3,7},{4,0},{5,1},{6,2},{7,3},{8,12},{9,13},{10,... | collective-permute-start | bytes 737288 | tf_op jit(solution)/shard_map/ppermute | solution.py:24
  115.2 24.1 %collective-permute-start.51 = (bf16[128,960]{1,0:T(8,128)(2,1)}, bf16[128,960]{1,0:T(8,128)(2,1)}, u32[]{:S(2)}, u32[]{:S(2)}) collective-permute-start(bf16[128,960]{1,0:T(8,128)(2,1)} %collective-permute-done.50), channel_id=1, source_target_pairs={{0,4},{1,5},{2,6},{3,7},{4,0},{5,1},{6,2},{7,3},{8,12},{9,13},{10,... | collective-permute-start | bytes 737288 | tf_op jit(solution)/shard_map/ppermute | solution.py:24
  115.2 29.7 %collective-permute-start.53 = (bf16[128,960]{1,0:T(8,128)(2,1)}, bf16[128,960]{1,0:T(8,128)(2,1)}, u32[]{:S(2)}, u32[]{:S(2)}) collective-permute-start(bf16[128,960]{1,0:T(8,128)(2,1)} %collective-permute-done.52), channel_id=1, source_target_pairs={{0,4},{1,5},{2,6},{3,7},{4,0},{5,1},{6,2},{7,3},{8,12},{9,13},{10,... | collective-permute-start | bytes 737288 | tf_op jit(solution)/shard_map/ppermute | solution.py:24
  135.0 17.7 %collective-permute-start.29 = (bf16[960,128]{1,0:T(8,128)(2,1)}, bf16[960,128]{1,0:T(8,128)(2,1)S(1)}, u32[]{:S(2)}, u32[]{:S(2)}) collective-permute-start(bf16[960,128]{1,0:T(8,128)(2,1)} %collective-permute-done.28), channel_id=1, source_target_pairs={{0,4},{1,5},{2,6},{3,7},{4,0},{5,1},{6,2},{7,3},{8,12},{9,13},{10,... | collective-permute-start | bytes 737288 | tf_op jit(solution)/shard_map/ppermute | solution.py:24
  135.1 20.8 %collective-permute-start.31 = (bf16[960,128]{1,0:T(8,128)(2,1)}, bf16[960,128]{1,0:T(8,128)(2,1)S(1)}, u32[]{:S(2)}, u32[]{:S(2)}) collective-permute-start(bf16[960,128]{1,0:T(8,128)(2,1)} %collective-permute-done.30), channel_id=1, source_target_pairs={{0,4},{1,5},{2,6},{3,7},{4,0},{5,1},{6,2},{7,3},{8,12},{9,13},{10,... | collective-permute-start | bytes 737288 | tf_op jit(solution)/shard_map/ppermute | solution.py:24
  135.6 21.4 %collective-permute-start.33 = (bf16[960,128]{1,0:T(8,128)(2,1)}, bf16[960,128]{1,0:T(8,128)(2,1)S(1)}, u32[]{:S(2)}, u32[]{:S(2)}) collective-permute-start(bf16[960,128]{1,0:T(8,128)(2,1)} %collective-permute-done.32), channel_id=1, source_target_pairs={{0,4},{1,5},{2,6},{3,7},{4,0},{5,1},{6,2},{7,3},{8,12},{9,13},{10,... | collective-permute-start | bytes 737288 | tf_op jit(solution)/shard_map/ppermute | solution.py:24
  139.3 18.2 %collective-permute-start.12 = (bf16[1024,128]{1,0:T(8,128)(2,1)S(1)}, bf16[1024,128]{1,0:T(8,128)(2,1)S(1)}, u32[]{:S(2)}, u32[]{:S(2)}) collective-permute-start(bf16[1024,128]{1,0:T(8,128)(2,1)S(1)} %get-tuple-element.188), channel_id=1, source_target_pairs={{0,3},{1,2},{2,1},{3,0},{4,7},{5,6},{6,5},{7,4},{8,11},{9,10},{10,... | collective-permute-start | bytes 786440 | tf_op jit(solution)/shard_map/ppermute | solution.py:24
  144.9 19.0 %collective-permute-start.11 = (bf16[1024,128]{1,0:T(8,128)(2,1)S(1)}, bf16[1024,128]{1,0:T(8,128)(2,1)S(1)}, u32[]{:S(2)}, u32[]{:S(2)}) collective-permute-start(bf16[1024,128]{1,0:T(8,128)(2,1)S(1)} %get-tuple-element.188), channel_id=1, source_target_pairs={{0,2},{1,3},{2,0},{3,1},{4,6},{5,7},{6,4},{7,5},{8,10},{9,11},{10,... | collective-permute-start | bytes 786440 | tf_op jit(solution)/shard_map/ppermute | solution.py:24
  152.7 14.1 %collective-permute-start.10 = (bf16[1024,128]{1,0:T(8,128)(2,1)S(1)}, bf16[1024,128]{1,0:T(8,128)(2,1)S(1)}, u32[]{:S(2)}, u32[]{:S(2)}) collective-permute-start(bf16[1024,128]{1,0:T(8,128)(2,1)S(1)} %get-tuple-element.188), channel_id=1, source_target_pairs={{0,1},{1,0},{2,3},{3,2},{4,5},{5,4},{6,7},{7,6},{8,9},{9,8},{10,11... | collective-permute-start | bytes 786440 | tf_op jit(solution)/shard_map/ppermute | solution.py:24
  197.9 14.2 %collective-permute-start.20 = (bf16[1024,128]{0,1:T(8,128)(2,1)}, bf16[1024,128]{0,1:T(8,128)(2,1)}, u32[]{:S(2)}, u32[]{:S(2)}) collective-permute-start(bf16[1024,128]{0,1:T(8,128)(2,1)} %convert_bitcast_fusion.5), channel_id=1, source_target_pairs={{0,16},{1,17},{2,18},{3,19},{4,20},{5,21},{6,22},{7,23},{8,24},{9,... | collective-permute-start | bytes 786440 | tf_op jit(solution)/shard_map/ppermute | solution.py:24
  198.3 15.0 %collective-permute-start.22 = (bf16[1024,128]{0,1:T(8,128)(2,1)}, bf16[1024,128]{0,1:T(8,128)(2,1)}, u32[]{:S(2)}, u32[]{:S(2)}) collective-permute-start(bf16[1024,128]{0,1:T(8,128)(2,1)} %convert_bitcast_fusion.5), channel_id=1, source_target_pairs={{0,24},{1,25},{2,26},{3,27},{4,28},{5,29},{6,30},{7,31},{8,16},{9,... | collective-permute-start | bytes 786440 | tf_op jit(solution)/shard_map/ppermute | solution.py:24
  268.9 39.5 %collective-permute-start.45 = (bf16[128,960]{0,1:T(8,128)(2,1)S(1)}, bf16[128,960]{0,1:T(8,128)(2,1)}, u32[]{:S(2)}, u32[]{:S(2)}) collective-permute-start(bf16[128,960]{0,1:T(8,128)(2,1)S(1)} %copy.401), channel_id=1, source_target_pairs={{0,4},{1,5},{2,6},{3,7},{4,0},{5,1},{6,2},{7,3},{8,12},{9,13},{10,... | collective-permute-start | bytes 737288 | tf_op jit(solution)/shard_map/ppermute | solution.py:24
  275.5 30.6 %collective-permute-start.111 = (bf16[80,960]{1,0:T(8,128)(2,1)}, bf16[80,960]{1,0:T(8,128)(2,1)}, u32[]{:S(2)}, u32[]{:S(2)}) collective-permute-start(bf16[80,960]{1,0:T(8,128)(2,1)} %get-tuple-element.163), channel_id=1, source_target_pairs={{0,3},{1,2},{2,1},{3,0},{4,7},{5,6},{6,5},{7,4},{8,11},{9,10},{10,... | collective-permute-start | bytes 460808 | tf_op jit(solution)/shard_map/ppermute | solution.py:24
  277.4 29.2 %collective-permute-start.110 = (bf16[80,960]{1,0:T(8,128)(2,1)}, bf16[80,960]{1,0:T(8,128)(2,1)}, u32[]{:S(2)}, u32[]{:S(2)}) collective-permute-start(bf16[80,960]{1,0:T(8,128)(2,1)} %get-tuple-element.164), channel_id=1, source_target_pairs={{0,2},{1,3},{2,0},{3,1},{4,6},{5,7},{6,4},{7,5},{8,10},{9,11},{10,... | collective-permute-start | bytes 460808 | tf_op jit(solution)/shard_map/ppermute | solution.py:24
  277.4 29.3 %collective-permute-start.109 = (bf16[80,960]{1,0:T(8,128)(2,1)}, bf16[80,960]{1,0:T(8,128)(2,1)}, u32[]{:S(2)}, u32[]{:S(2)}) collective-permute-start(bf16[80,960]{1,0:T(8,128)(2,1)} %get-tuple-element.162), channel_id=1, source_target_pairs={{0,1},{1,0},{2,3},{3,2},{4,5},{5,4},{6,7},{7,6},{8,9},{9,8},{10,11... | collective-permute-start | bytes 460808 | tf_op jit(solution)/shard_map/ppermute | solution.py:24
  284.7 25.8 %collective-permute-start.43 = (bf16[128,960]{0,1:T(8,128)(2,1)}, bf16[128,960]{0,1:T(8,128)(2,1)}, u32[]{:S(2)}, u32[]{:S(2)}) collective-permute-start(bf16[128,960]{0,1:T(8,128)(2,1)} %copy.399), channel_id=1, source_target_pairs={{0,4},{1,5},{2,6},{3,7},{4,0},{5,1},{6,2},{7,3},{8,12},{9,13},{10,... | collective-permute-start | bytes 737288 | tf_op jit(solution)/shard_map/ppermute | solution.py:24
  306.6 65.2 %collective-permute-start.40 = (bf16[128,960]{0,1:T(8,128)(2,1)}, bf16[128,960]{0,1:T(8,128)(2,1)}, u32[]{:S(2)}, u32[]{:S(2)}) collective-permute-start(bf16[128,960]{0,1:T(8,128)(2,1)} %copy.395), channel_id=1, source_target_pairs={{0,4},{1,5},{2,6},{3,7},{4,0},{5,1},{6,2},{7,3},{8,12},{9,13},{10,... | collective-permute-start | bytes 737288 | tf_op jit(solution)/shard_map/ppermute | solution.py:24
  312.6 12.5 %collective-permute-start.101 = (bf16[240,640]{0,1:T(8,128)(2,1)S(1)}, bf16[240,640]{0,1:T(8,128)(2,1)S(1)}, u32[]{:S(2)}, u32[]{:S(2)}) collective-permute-start(bf16[240,640]{0,1:T(8,128)(2,1)S(1)} %bitcast.567), channel_id=1, source_target_pairs={{0,3},{1,2},{2,1},{3,0},{4,7},{5,6},{6,5},{7,4},{8,11},{9,10},{10,... | collective-permute-start | bytes 921608 | tf_op jit(solution)/shard_map/ppermute | solution.py:24
  315.2 27.6 %collective-permute-start.100 = (bf16[240,640]{0,1:T(8,128)(2,1)S(1)}, bf16[240,640]{0,1:T(8,128)(2,1)S(1)}, u32[]{:S(2)}, u32[]{:S(2)}) collective-permute-start(bf16[240,640]{0,1:T(8,128)(2,1)S(1)} %bitcast.566), channel_id=1, source_target_pairs={{0,2},{1,3},{2,0},{3,1},{4,6},{5,7},{6,4},{7,5},{8,10},{9,11},{10,... | collective-permute-start | bytes 921608 | tf_op jit(solution)/shard_map/ppermute | solution.py:24
  316.0 27.3 %collective-permute-start.99 = (bf16[240,640]{0,1:T(8,128)(2,1)S(1)}, bf16[240,640]{0,1:T(8,128)(2,1)S(1)}, u32[]{:S(2)}, u32[]{:S(2)}) collective-permute-start(bf16[240,640]{0,1:T(8,128)(2,1)S(1)} %bitcast.565), channel_id=1, source_target_pairs={{0,1},{1,0},{2,3},{3,2},{4,5},{5,4},{6,7},{7,6},{8,9},{9,8},{10,11... | collective-permute-start | bytes 921608 | tf_op jit(solution)/shard_map/ppermute | solution.py:24
  320.6 24.1 %collective-permute-start.113 = (bf16[80,960]{1,0:T(8,128)(2,1)S(1)}, bf16[80,960]{1,0:T(8,128)(2,1)S(1)}, u32[]{:S(2)}, u32[]{:S(2)}) collective-permute-start(bf16[80,960]{1,0:T(8,128)(2,1)S(1)} %get-tuple-element.107), channel_id=1, source_target_pairs={{0,8},{1,9},{2,10},{3,11},{4,12},{5,13},{6,14},{7,15},{8,0},{9,1},... | collective-permute-start | bytes 460808 | tf_op jit(solution)/shard_map/ppermute | solution.py:24
  325.1 40.1 %collective-permute-start.54 = (bf16[128,960]{0,1:T(8,128)(2,1)}, bf16[128,960]{0,1:T(8,128)(2,1)S(1)}, u32[]{:S(2)}, u32[]{:S(2)}) collective-permute-start(bf16[128,960]{0,1:T(8,128)(2,1)} %copy.411), channel_id=1, source_target_pairs={{0,4},{1,5},{2,6},{3,7},{4,0},{5,1},{6,2},{7,3},{8,12},{9,13},{10,... | collective-permute-start | bytes 737288 | tf_op jit(solution)/shard_map/ppermute | solution.py:24
  351.8 14.6 %collective-permute-start.60 = (bf16[128,960]{0,1:T(8,128)(2,1)}, bf16[128,960]{0,1:T(8,128)(2,1)S(1)}, u32[]{:S(2)}, u32[]{:S(2)}) collective-permute-start(bf16[128,960]{0,1:T(8,128)(2,1)} %add_convert_fusion.4), channel_id=1, source_target_pairs={{0,24},{1,25},{2,26},{3,27},{4,28},{5,29},{6,30},{7,31},{8,16},{9,... | collective-permute-start | bytes 737288 | tf_op jit(solution)/shard_map/ppermute | solution.py:24
  351.9 15.2 %collective-permute-start.58 = (bf16[128,960]{0,1:T(8,128)(2,1)}, bf16[128,960]{0,1:T(8,128)(2,1)S(1)}, u32[]{:S(2)}, u32[]{:S(2)}) collective-permute-start(bf16[128,960]{0,1:T(8,128)(2,1)} %add_convert_fusion.5), channel_id=1, source_target_pairs={{0,16},{1,17},{2,18},{3,19},{4,20},{5,21},{6,22},{7,23},{8,24},{9,... | collective-permute-start | bytes 737288 | tf_op jit(solution)/shard_map/ppermute | solution.py:24
  355.1 13.7 %collective-permute-start.56 = (bf16[128,960]{0,1:T(8,128)(2,1)}, bf16[128,960]{0,1:T(8,128)(2,1)S(1)}, u32[]{:S(2)}, u32[]{:S(2)}) collective-permute-start(bf16[128,960]{0,1:T(8,128)(2,1)} %add_convert_fusion.6), channel_id=1, source_target_pairs={{0,8},{1,9},{2,10},{3,11},{4,12},{5,13},{6,14},{7,15},{8,0},{9,1},... | collective-permute-start | bytes 737288 | tf_op jit(solution)/shard_map/ppermute | solution.py:24
  366.4 13.3 %collective-permute-start.44 = (bf16[128,960]{0,1:T(8,128)(2,1)}, bf16[128,960]{0,1:T(8,128)(2,1)}, u32[]{:S(2)}, u32[]{:S(2)}) collective-permute-start(bf16[128,960]{0,1:T(8,128)(2,1)} %add_convert_fusion.8), channel_id=1, source_target_pairs={{0,16},{1,17},{2,18},{3,19},{4,20},{5,21},{6,22},{7,23},{8,24},{9,... | collective-permute-start | bytes 737288 | tf_op jit(solution)/shard_map/ppermute | solution.py:24
  367.1 13.3 %collective-permute-start.42 = (bf16[128,960]{0,1:T(8,128)(2,1)}, bf16[128,960]{0,1:T(8,128)(2,1)}, u32[]{:S(2)}, u32[]{:S(2)}) collective-permute-start(bf16[128,960]{0,1:T(8,128)(2,1)} %add_convert_fusion.9), channel_id=1, source_target_pairs={{0,8},{1,9},{2,10},{3,11},{4,12},{5,13},{6,14},{7,15},{8,0},{9,1},... | collective-permute-start | bytes 737288 | tf_op jit(solution)/shard_map/ppermute | solution.py:24
  368.8 19.2 %collective-permute-start.102 = (bf16[240,640]{0,1:T(8,128)(2,1)S(1)}, bf16[240,640]{0,1:T(8,128)(2,1)}, u32[]{:S(2)}, u32[]{:S(2)}) collective-permute-start(bf16[240,640]{0,1:T(8,128)(2,1)S(1)} %get-tuple-element.109), channel_id=1, source_target_pairs={{0,4},{1,5},{2,6},{3,7},{4,0},{5,1},{6,2},{7,3},{8,12},{9,13},{10,... | collective-permute-start | bytes 921608 | tf_op jit(solution)/shard_map/ppermute | solution.py:24
  371.8 18.9 %collective-permute-start.103 = (bf16[240,640]{0,1:T(8,128)(2,1)S(1)}, bf16[240,640]{0,1:T(8,128)(2,1)}, u32[]{:S(2)}, u32[]{:S(2)}) collective-permute-start(bf16[240,640]{0,1:T(8,128)(2,1)S(1)} %get-tuple-element.109), channel_id=1, source_target_pairs={{0,8},{1,9},{2,10},{3,11},{4,12},{5,13},{6,14},{7,15},{8,0},{9,1},... | collective-permute-start | bytes 921608 | tf_op jit(solution)/shard_map/ppermute | solution.py:24
  375.3 57.3 %collective-permute-start.105 = (bf16[240,640]{0,1:T(8,128)(2,1)S(1)}, bf16[240,640]{0,1:T(8,128)(2,1)}, u32[]{:S(2)}, u32[]{:S(2)}) collective-permute-start(bf16[240,640]{0,1:T(8,128)(2,1)S(1)} %get-tuple-element.109), channel_id=1, source_target_pairs={{0,16},{1,17},{2,18},{3,19},{4,20},{5,21},{6,22},{7,23},{8,24},{9,... | collective-permute-start | bytes 921608 | tf_op jit(solution)/shard_map/ppermute | solution.py:24
  382.7 50.0 %collective-permute-start.107 = (bf16[240,640]{0,1:T(8,128)(2,1)S(1)}, bf16[240,640]{0,1:T(8,128)(2,1)}, u32[]{:S(2)}, u32[]{:S(2)}) collective-permute-start(bf16[240,640]{0,1:T(8,128)(2,1)S(1)} %get-tuple-element.109), channel_id=1, source_target_pairs={{0,24},{1,25},{2,26},{3,27},{4,28},{5,29},{6,30},{7,31},{8,16},{9,... | collective-permute-start | bytes 921608 | tf_op jit(solution)/shard_map/ppermute | solution.py:24
  402.8 30.4 %collective-permute-start.91 = (bf16[240,128]{1,0:T(8,128)(2,1)S(1)}, bf16[240,128]{1,0:T(8,128)(2,1)S(1)}, u32[]{:S(2)}, u32[]{:S(2)}) collective-permute-start(bf16[240,128]{1,0:T(8,128)(2,1)S(1)} %get-tuple-element.199), channel_id=1, source_target_pairs={{0,3},{1,2},{2,1},{3,0},{4,7},{5,6},{6,5},{7,4},{8,11},{9,10},{10,... | collective-permute-start | bytes 184328 | tf_op jit(solution)/shard_map/ppermute | solution.py:24
  404.7 28.5 %collective-permute-start.90 = (bf16[240,128]{1,0:T(8,128)(2,1)S(1)}, bf16[240,128]{1,0:T(8,128)(2,1)S(1)}, u32[]{:S(2)}, u32[]{:S(2)}) collective-permute-start(bf16[240,128]{1,0:T(8,128)(2,1)S(1)} %get-tuple-element.200), channel_id=1, source_target_pairs={{0,2},{1,3},{2,0},{3,1},{4,6},{5,7},{6,4},{7,5},{8,10},{9,11},{10,... | collective-permute-start | bytes 184328 | tf_op jit(solution)/shard_map/ppermute | solution.py:24
  404.7 28.5 %collective-permute-start.89 = (bf16[240,128]{1,0:T(8,128)(2,1)S(1)}, bf16[240,128]{1,0:T(8,128)(2,1)S(1)}, u32[]{:S(2)}, u32[]{:S(2)}) collective-permute-start(bf16[240,128]{1,0:T(8,128)(2,1)S(1)} %get-tuple-element.198), channel_id=1, source_target_pairs={{0,1},{1,0},{2,3},{3,2},{4,5},{5,4},{6,7},{7,6},{8,9},{9,8},{10,11... | collective-permute-start | bytes 184328 | tf_op jit(solution)/shard_map/ppermute | solution.py:24
  432.6 17.0 %collective-permute-start.104 = (bf16[240,640]{0,1:T(8,128)(2,1)}, bf16[240,640]{0,1:T(8,128)(2,1)}, u32[]{:S(2)}, u32[]{:S(2)}) collective-permute-start(bf16[240,640]{0,1:T(8,128)(2,1)} %collective-permute-done.103), channel_id=1, source_target_pairs={{0,4},{1,5},{2,6},{3,7},{4,0},{5,1},{6,2},{7,3},{8,12},{9,13},{10,... | collective-permute-start | bytes 921608 | tf_op jit(solution)/shard_map/ppermute | solution.py:24
  432.7 18.9 %collective-permute-start.106 = (bf16[240,640]{0,1:T(8,128)(2,1)}, bf16[240,640]{0,1:T(8,128)(2,1)S(1)}, u32[]{:S(2)}, u32[]{:S(2)}) collective-permute-start(bf16[240,640]{0,1:T(8,128)(2,1)} %collective-permute-done.105), channel_id=1, source_target_pairs={{0,4},{1,5},{2,6},{3,7},{4,0},{5,1},{6,2},{7,3},{8,12},{9,13},{10,... | collective-permute-start | bytes 921608 | tf_op jit(solution)/shard_map/ppermute | solution.py:24
  433.2 19.4 %collective-permute-start.108 = (bf16[240,640]{0,1:T(8,128)(2,1)}, bf16[240,640]{0,1:T(8,128)(2,1)S(1)}, u32[]{:S(2)}, u32[]{:S(2)}) collective-permute-start(bf16[240,640]{0,1:T(8,128)(2,1)} %collective-permute-done.107), channel_id=1, source_target_pairs={{0,4},{1,5},{2,6},{3,7},{4,0},{5,1},{6,2},{7,3},{8,12},{9,13},{10,... | collective-permute-start | bytes 921608 | tf_op jit(solution)/shard_map/ppermute | solution.py:24
  456.8 17.9 %collective-permute-start.71 = (bf16[1024,128]{1,0:T(8,128)(2,1)S(1)}, bf16[1024,128]{1,0:T(8,128)(2,1)S(1)}, u32[]{:S(2)}, u32[]{:S(2)}) collective-permute-start(bf16[1024,128]{1,0:T(8,128)(2,1)S(1)} %get-tuple-element.181), channel_id=1, source_target_pairs={{0,3},{1,2},{2,1},{3,0},{4,7},{5,6},{6,5},{7,4},{8,11},{9,10},{10,... | collective-permute-start | bytes 786440 | tf_op jit(solution)/shard_map/ppermute | solution.py:24
  459.1 22.5 %collective-permute-start.70 = (bf16[1024,128]{1,0:T(8,128)(2,1)S(1)}, bf16[1024,128]{1,0:T(8,128)(2,1)S(1)}, u32[]{:S(2)}, u32[]{:S(2)}) collective-permute-start(bf16[1024,128]{1,0:T(8,128)(2,1)S(1)} %get-tuple-element.182), channel_id=1, source_target_pairs={{0,2},{1,3},{2,0},{3,1},{4,6},{5,7},{6,4},{7,5},{8,10},{9,11},{10,... | collective-permute-start | bytes 786440 | tf_op jit(solution)/shard_map/ppermute | solution.py:24
  459.1 22.5 %collective-permute-start.69 = (bf16[1024,128]{1,0:T(8,128)(2,1)S(1)}, bf16[1024,128]{1,0:T(8,128)(2,1)S(1)}, u32[]{:S(2)}, u32[]{:S(2)}) collective-permute-start(bf16[1024,128]{1,0:T(8,128)(2,1)S(1)} %get-tuple-element.180), channel_id=1, source_target_pairs={{0,1},{1,0},{2,3},{3,2},{4,5},{5,4},{6,7},{7,6},{8,9},{9,8},{10,11... | collective-permute-start | bytes 786440 | tf_op jit(solution)/shard_map/ppermute | solution.py:24
  504.4 19.0 %collective-permute-start.77 = (bf16[128,960]{0,1:T(8,128)(2,1)}, bf16[128,960]{0,1:T(8,128)(2,1)}, u32[]{:S(2)}, u32[]{:S(2)}) collective-permute-start(bf16[128,960]{0,1:T(8,128)(2,1)} %copy.437), channel_id=1, source_target_pairs={{0,4},{1,5},{2,6},{3,7},{4,0},{5,1},{6,2},{7,3},{8,12},{9,13},{10,... | collective-permute-start | bytes 737288 | tf_op jit(solution)/shard_map/ppermute | solution.py:24
  508.1 11.5 %collective-permute-start.81 = (bf16[256,256]{1,0:T(8,128)(2,1)}, bf16[256,256]{1,0:T(8,128)(2,1)S(1)}, u32[]{:S(2)}, u32[]{:S(2)}) collective-permute-start(bf16[256,256]{1,0:T(8,128)(2,1)} %get-tuple-element.178), channel_id=1, source_target_pairs={{0,3},{1,2},{2,1},{3,0},{4,7},{5,6},{6,5},{7,4},{8,11},{9,10},{10,... | collective-permute-start | bytes 393224 | tf_op jit(solution)/shard_map/ppermute | solution.py:24
  510.2 11.5 %collective-permute-start.79 = (bf16[256,256]{1,0:T(8,128)(2,1)}, bf16[256,256]{1,0:T(8,128)(2,1)}, u32[]{:S(2)}, u32[]{:S(2)}) collective-permute-start(bf16[256,256]{1,0:T(8,128)(2,1)} %get-tuple-element.177), channel_id=1, source_target_pairs={{0,1},{1,0},{2,3},{3,2},{4,5},{5,4},{6,7},{7,6},{8,9},{9,8},{10,11... | collective-permute-start | bytes 393224 | tf_op jit(solution)/shard_map/ppermute | solution.py:24
  521.7 21.0 %collective-permute-start.72 = (bf16[128,960]{0,1:T(8,128)(2,1)}, bf16[128,960]{0,1:T(8,128)(2,1)S(1)}, u32[]{:S(2)}, u32[]{:S(2)}) collective-permute-start(bf16[128,960]{0,1:T(8,128)(2,1)} %copy.431), channel_id=1, source_target_pairs={{0,4},{1,5},{2,6},{3,7},{4,0},{5,1},{6,2},{7,3},{8,12},{9,13},{10,... | collective-permute-start | bytes 737288 | tf_op jit(solution)/shard_map/ppermute | solution.py:24
  533.3 12.8 %collective-permute-start.76 = (bf16[128,960]{0,1:T(8,128)(2,1)}, bf16[128,960]{0,1:T(8,128)(2,1)}, u32[]{:S(2)}, u32[]{:S(2)}) collective-permute-start(bf16[128,960]{0,1:T(8,128)(2,1)} %add_convert_fusion.2), channel_id=1, source_target_pairs={{0,16},{1,17},{2,18},{3,19},{4,20},{5,21},{6,22},{7,23},{8,24},{9,... | collective-permute-start | bytes 737288 | tf_op jit(solution)/shard_map/ppermute | solution.py:24
  (158 other events, 2050.8 us)
